TPU v7x, 1024 devices: a whole 4x4x32 slice. The times are simulated.
1024 devices in a mesh: row: 64 (over x, z_lo, core), col: 16 (over y, z_hi).
Axes of the slice: x: 4, y: 4, z: 32 (z_hi: 4, z_lo: 8; z = z_hi * 8 + z_lo), core: 2. Of those that a mesh axis runs over, the one named last changes fastest.
Arguments:
- features: bfloat16 [262144, 128], P(('col', 'row')), may hold values from -6 to 6
- adj_blocks: bfloat16 [64, 16, 64, 128, 128], P('row', 'col'), may hold values from -0.09375 to 0.09375
- block_coords: int32 [64, 16, 2, 64], P('row', 'col'), may hold values from 0 to 127, as said below
- counts: int32 [64, 16], replicated, may hold values from 4 to 64, as said below
- weight: bfloat16 [128, 256], replicated, may hold values from -0.5 to 0.5
- cotangent: bfloat16 [262144, 256], P(('row', 'col')), may hold values from -0.01171875 to 0.01171875
Outputs:
- activated: bfloat16 [262144, 256], P(('row', 'col'))
- weight_grad: float32 [128, 256], replicated
Inputs may be any that keep to these rules, and one draw needn't show every extreme that they name: `block_coords`: slots at or past a tile's count hold values that take no part. `block_coords`: block rows are below 32, block columns below 128. `counts`: each count is 64 divided by a power of two.
All inputs are finite; a program needn't handle non-finite values.
Results may differ from a plain program's by a relative error of at most 0.0052.
Values may be sent and summed in bfloat16 or wider, within the bound.
A program may use at most 32 MiB of HBM per device.

v0:
```python
import jax
import jax.numpy as jnp
from jax import lax
from jax.sharding import PartitionSpec as P

GROUP = 32


def silu_slope(preact, sigmoid_value):
    return sigmoid_value * (1.0 + preact * (1.0 - sigmoid_value))


def add_blocks(partial_value, chosen, target_rows, inputs, alive_mask):
    products = jnp.einsum("gab,gbf->gaf", chosen, inputs, preferred_element_type=jnp.float32)
    products = jnp.where(alive_mask[:, None, None], products, 0.0)
    return partial_value.at[target_rows].add(products)


def body(features, adj_blocks, block_coords, counts, weight, cotangent):
    tile_blocks = adj_blocks[0, 0]
    tile_coords = block_coords[0, 0]
    slot_count, block_size = (tile_blocks.shape[0], tile_blocks.shape[1])
    feature_width = features.shape[1]
    row_blocks = features.shape[0] * lax.axis_size("col") // block_size
    row_index = lax.axis_index("row")
    col_index = lax.axis_index("col")
    live_count = counts[row_index, col_index]
    running = jnp.zeros((row_blocks, block_size, feature_width), jnp.float32)
    gathered = lax.all_gather(features, "row", axis=0, tiled=True)
    feature_blocks = gathered.reshape(gathered.shape[0] // block_size, block_size, feature_width)

    def advance(turn_index, partial_value):
        first_slot = turn_index * GROUP
        alive_mask = first_slot + jnp.arange(GROUP, dtype=jnp.int32) < live_count
        chosen = lax.dynamic_slice_in_dim(tile_blocks, first_slot, GROUP, 0)
        target_rows = lax.dynamic_slice_in_dim(tile_coords[0], first_slot, GROUP, 0)
        source_cols = lax.dynamic_slice_in_dim(tile_coords[1], first_slot, GROUP, 0)
        inputs = jnp.take(feature_blocks, source_cols, axis=0)
        return add_blocks(partial_value, chosen, target_rows, inputs, alive_mask)

    turns = (live_count + GROUP - 1) // GROUP
    running = lax.fori_loop(0, turns, advance, running)
    partial_rows = running.reshape(row_blocks * block_size, feature_width)
    aggregate = lax.psum_scatter(partial_rows, "col", scatter_dimension=0, tiled=True)
    rounded = aggregate.astype(jnp.bfloat16)
    preact = jnp.dot(rounded, weight, preferred_element_type=jnp.float32)
    sigmoid_value = jax.nn.sigmoid(preact)
    activated = (preact * sigmoid_value).astype(jnp.bfloat16)
    slope_grad = (cotangent.astype(jnp.float32) * silu_slope(preact, sigmoid_value)).astype(
        jnp.bfloat16
    )
    local_grad = lax.dot_general(
        rounded, slope_grad, (((0,), (0,)), ((), ())), preferred_element_type=jnp.float32
    )
    weight_grad = lax.psum(local_grad, ("row", "col"))
    return (activated, weight_grad)


def solution(mesh):
    return jax.shard_map(
        body,
        mesh=mesh,
        in_specs=(
            P(("col", "row"), None),
            P("row", "col", None, None, None),
            P("row", "col", None, None),
            P(),
            P(),
            P(("row", "col"), None),
        ),
        out_specs=(P(("row", "col"), None), P()),
        check_vma=False,
    )
```

profile of v0, /device:TPU:1, one launch (start us, length us, event | category | flops | bytes accessed | tf_op | source)
XLA Modules:
  0.0 1243.8 jit_solution(17164337222921746499)
XLA Ops:
  7.2 0.0 copy-start
  7.2 0.0 copy-start.1
  7.2 0.0 all-gather.2.cloned.1.call-start
  7.2 0.7 all-gather.2.cloned.1.call-update
  7.9 0.0 reduce-scatter.2.cloned.1.call-start
  8.0 1.3 dynamic_slice.18
  9.9 142.4 %all-gather.2.cloned.1.call-done = bf16[16384,128]{1,0:T(8,128)(2,1)} async-done(((bf16[256,128]{1,0:T(8,128)(2,1)}), bf16[16384,128]{1,0:T(8,128)(2,1)}) %all-gather.2.cloned.1.call-update) | async-done | bytes 4194320 | tf_op jit(solution)/shard_map/all_gather | solution.py:29
  152.3 1.6 broadcast_in_dim.27
  153.9 0.0 copy-done.1
  153.9 11.7 while.10
  153.9 0.1 fusion.23
  154.0 0.7 compare_and_fusion.2
  154.7 2.9 gather_fusion
  157.7 1.7 convolution_select_fusion.2
  159.4 6.2 scatter_fusion
  165.6 0.0 copy-start.2
  165.6 0.0 reduce-scatter.2.cloned.1.call-update
  165.6 0.0 all-reduce.2.cloned.1.call-start
  165.6 220.8 %reduce-scatter.2.cloned.1.call-done = f32[256,128]{1,0:T(8,128)} async-done(((f32[4096,128]{1,0:T(8,128)}), f32[256,128]{1,0:T(8,128)}) %reduce-scatter.2.cloned.1.call-update) | async-done | bytes 131088 | tf_op jit(solution)/shard_map/reduce_scatter | solution.py:44
  386.5 0.0 copy-done
  386.5 1.8 multiply_convert_fusion.1
  388.2 0.0 copy-done.2
  388.2 1.8 fusion.9
  390.1 0.0 all-reduce.2.cloned.1.call-update
  390.1 845.7 %all-reduce.2.cloned.1.call-done = f32[128,256]{1,0:T(8,128)} async-done(((f32[128,256]{1,0:T(8,128)}), f32[128,256]{1,0:T(8,128)}) %all-reduce.2.cloned.1.call-update) | async-done | bytes 131088 | tf_op jit(solution)/shard_map/psum | solution.py:55
  1235.8 1.6 copy.16
  (2 shorter events, 0.0 us)
Async XLA Ops:
  7.2 379.3 %copy-start = (bf16[128,256]{1,0:T(8,128)(2,1)S(1)}, bf16[128,256]{1,0:T(8,128)(2,1)}, u32[]{:S(2)}) copy-start(bf16[128,256]{1,0:T(8,128)(2,1)} %param.12) | copy-start | bytes 196612
  7.2 146.7 %copy-start.1 = (s32[1,1,2,64]{3,2,1,0:T(2,128)S(1)}, s32[1,1,2,64]{3,2,1,0:T(2,128)}, u32[]{:S(2)}) copy-start(s32[1,1,2,64]{3,2,1,0:T(2,128)} %param.10) | copy-start | bytes 1540
  7.2 145.1 %all-gather.2.cloned.1.call-start = ((), (), s32[]{:S(2)}) async-start(), calls=%async_computation.1 | async-start | bytes 4259840 | tf_op jit(solution)/shard_map/all_gather | solution.py:29
  7.9 378.5 %reduce-scatter.2.cloned.1.call-start = ((), (), s32[]{:S(2)}) async-start(), calls=%async_computation.2 | async-start | bytes 2228224 | tf_op jit(solution)/shard_map/reduce_scatter | solution.py:44
  165.6 222.7 %copy-start.2 = (bf16[256,256]{1,0:T(8,128)(2,1)S(1)}, bf16[256,256]{1,0:T(8,128)(2,1)}, u32[]{:S(2)}) copy-start(bf16[256,256]{1,0:T(8,128)(2,1)} %param.13) | copy-start | bytes 393220
  165.6 1070.2 %all-reduce.2.cloned.1.call-start = ((), (), s32[]{:S(2)}) async-start(), calls=%async_computation.3 | async-start | bytes 262144 | tf_op jit(solution)/shard_map/psum | solution.py:55
Sparse Core Ops, SparseCore 0:
  10.8 141.5 all-gather.1
  165.7 220.7 reduce-scatter.1
  393.4 842.3 all-reduce.1
where the time goes:
time: 1240 us
  waiting for transfers between devices  1210 us (98%)
  between operations  14.4 us (1%)
    psum x1, waiting for transfers between devices, body(): weight_grad = lax.psum(local_grad, ('row', 'col'))  846 us
    reduce_scatter x1, waiting for transfers between devices, body(): lax.psum_scatter(partial_rows, 'col', scatter_dimension=0, tiled=True)  221 us
    all_gather x1, waiting for transfers between devices, body(): gathered = lax.all_gather(features, 'row', axis=0, tiled=True)  142 us
  transfers between devices with their start and end apart: 3, of which 3 were waited for; matrix products, arithmetic and copies ran while one was open for 0% of the time, Pallas kernels for 0%

commit v1 on v0

v1 whole, which is shorter than its diff:
```python
import jax
import jax.numpy as jnp
from jax import lax
from jax.experimental import pallas as pl
from jax.experimental.pallas import tpu as pltpu
from jax.sharding import PartitionSpec as P

NX, NZ, NC = 4, 8, 2
NY, NH = 4, 4
BLOCK = 128
GROUP = 4
MESH = pl.DeviceIdType.MESH


def remote(src, dst, send_sem, recv_sem, device):
    return pltpu.make_async_remote_copy(
        src_ref=src, dst_ref=dst, send_sem=send_sem, recv_sem=recv_sem, device_id=device, device_id_type=MESH
    )


def gather_kernel(
    f_ref, out_ref, own_sem, zu_s, zu_r, zd_s, zd_r, xs_s, xs_r, xf_s, xf_r, cc_s, cc_r
):
    half = f_ref.shape[0] // 2
    r = lax.axis_index("row")
    x, z, core = r // (NZ * NC), (r // NC) % NZ, r % NC

    def slot(xx, zz, cc=None):
        return ((xx % NX) * NZ + zz) * NC + (core if cc is None else cc)

    up, down = {"row": slot(x, z + 1)}, {"row": slot(x, z - 1)}
    right, left = {"row": slot(x + 1, z)}, {"row": slot(x - 1, z)}
    other = {"row": slot(x, z, 1 - core)}

    def z_up(d, src=None):
        s = slot(x, z - d)
        return remote(out_ref.at[s] if src is None else src, out_ref.at[s], zu_s.at[d], zu_r.at[d], up)

    def z_down(d, src=None):
        s = slot(x, z + d)
        return remote(out_ref.at[s] if src is None else src, out_ref.at[s], zd_s.at[d], zd_r.at[d], down)

    def x_copy(zz, way, src=None):
        s = slot(x, zz)
        return remote(
            out_ref.at[s] if src is None else src,
            out_ref.at[s],
            xs_s.at[way, zz],
            xs_r.at[way, zz],
            right if way == 0 else left,
        )

    def x_forward(zz, way):
        s = slot(x - 1 if way == 0 else x + 1, zz)
        rows = pl.ds(way * half, half)
        return remote(
            out_ref.at[s, rows],
            out_ref.at[s, rows],
            xf_s.at[way, zz],
            xf_r.at[way, zz],
            right if way == 0 else left,
        )

    def x_arrival(zz, way):
        s = slot(x - 1 if way == 0 else x + 1, zz)
        return remote(out_ref.at[s], out_ref.at[s], xs_s.at[way, zz], xs_r.at[way, zz], right)

    def f_arrival(zz, way):
        s = slot(x + 2, zz)
        rows = pl.ds(way * half, half)
        return remote(out_ref.at[s, rows], out_ref.at[s, rows], xf_s.at[way, zz], xf_r.at[way, zz], right)

    def cross(dx, zz, src=None):
        s = slot(x + dx, zz)
        return remote(out_ref.at[s] if src is None else src, out_ref.at[s], cc_s.at[dx, zz], cc_r.at[dx, zz], other)

    def cross_arrival(dx, zz):
        s = slot(x + dx, zz, 1 - core)
        return remote(out_ref.at[s], out_ref.at[s], cc_s.at[dx, zz], cc_r.at[dx, zz], other)

    has_up, has_down = z < NZ - 1, z > 0
    barrier = pltpu.get_barrier_semaphore()
    for device in (right, left, other):
        pl.semaphore_signal(barrier, inc=1, device_id=device, device_id_type=MESH)

    @pl.when(has_up)
    def _():
        pl.semaphore_signal(barrier, inc=1, device_id=up, device_id_type=MESH)

    @pl.when(has_down)
    def _():
        pl.semaphore_signal(barrier, inc=1, device_id=down, device_id_type=MESH)

    own = pltpu.make_async_copy(f_ref, out_ref.at[r], own_sem)
    own.start()
    pl.semaphore_wait(barrier, 3 + has_up.astype(jnp.int32) + has_down.astype(jnp.int32))

    pl.when(has_up)(lambda: z_up(0, f_ref).start())
    pl.when(has_down)(lambda: z_down(0, f_ref).start())
    x_copy(z, 0, f_ref).start()
    x_copy(z, 1, f_ref).start()
    cross(0, z, f_ref).start()

    def along_z(d, carry):
        @pl.when(z - d >= 0)
        def _():
            zz = z - d
            z_up_arrival = remote(
                out_ref.at[slot(x, zz)], out_ref.at[slot(x, zz)], zu_s.at[d - 1], zu_r.at[d - 1], other
            )
            z_up_arrival.wait_recv()
            pl.when(has_up)(lambda: z_up(d).start())
            x_copy(zz, 0).start()
            x_copy(zz, 1).start()
            cross(0, zz).start()

        @pl.when(z + d < NZ)
        def _():
            zz = z + d
            z_down_arrival = remote(
                out_ref.at[slot(x, zz)], out_ref.at[slot(x, zz)], zd_s.at[d - 1], zd_r.at[d - 1], other
            )
            z_down_arrival.wait_recv()
            pl.when(has_down)(lambda: z_down(d).start())
            x_copy(zz, 0).start()
            x_copy(zz, 1).start()
            cross(0, zz).start()

        return carry

    lax.fori_loop(1, NZ, along_z, 0)

    def along_x(zz):
        x_arrival(zz, 0).wait_recv()
        x_forward(zz, 0).start()
        cross(NX - 1, zz).start()
        x_arrival(zz, 1).wait_recv()
        x_forward(zz, 1).start()
        cross(1, zz).start()

    along_x(z)

    def along_x_step(d, carry):
        pl.when(z - d >= 0)(lambda: along_x(z - d))
        pl.when(z + d < NZ)(lambda: along_x(z + d))
        return carry

    lax.fori_loop(1, NZ, along_x_step, 0)

    def last_halves(zz):
        f_arrival(zz, 0).wait_recv()
        f_arrival(zz, 1).wait_recv()
        cross(2, zz).start()

    last_halves(z)

    def last_step(d, carry):
        pl.when(z - d >= 0)(lambda: last_halves(z - d))
        pl.when(z + d < NZ)(lambda: last_halves(z + d))
        return carry

    lax.fori_loop(1, NZ, last_step, 0)

    def drain(zz, carry):
        for dx in range(NX):
            cross_arrival(dx, zz).wait_recv()
            cross(dx, zz).wait_send()
        for way in range(2):
            x_copy(zz, way).wait_send()
            x_forward(zz, way).wait_send()
        pl.when(jnp.logical_and(has_up, zz <= z))(lambda: z_up(zz).wait_send())
        pl.when(jnp.logical_and(has_down, zz <= NZ - 1 - z))(lambda: z_down(zz).wait_send())
        return carry

    lax.fori_loop(0, NZ, drain, 0)
    own.wait()


def gather_features(features):
    rows, width = features.shape
    devices = NX * NZ * NC
    dma = pltpu.SemaphoreType.DMA
    return pl.pallas_call(
        gather_kernel,
        out_shape=jax.ShapeDtypeStruct((devices, rows, width), features.dtype),
        in_specs=[pl.BlockSpec(memory_space=pl.ANY)],
        out_specs=pl.BlockSpec(memory_space=pl.ANY),
        scratch_shapes=[dma]
        + [dma((NZ,))] * 4
        + [dma((2, NZ))] * 4
        + [dma((NX, NZ))] * 2,
        compiler_params=pltpu.CompilerParams(collective_id=0, has_side_effects=True),
        name="gather_features",
    )(features)


def multiply_kernel(coords_ref, counts_ref, adj_ref, feat_ref, out_ref, adj_v, feat_v, adj_sem, feat_sem):
    turns = counts_ref[lax.axis_index("row"), lax.axis_index("col")] // GROUP
    feat = pltpu.make_async_copy(feat_ref, feat_v, feat_sem)
    feat.start()

    def adj(g):
        slots = pl.ds(g * GROUP, GROUP)
        return pltpu.make_async_copy(adj_ref.at[slots], adj_v.at[slots], adj_sem.at[g])

    def fetch(g, carry):
        adj(g).start()
        return carry

    lax.fori_loop(0, turns, fetch, 0)
    out_ref[...] = jnp.zeros_like(out_ref)
    feat.wait()

    def turn(g, carry):
        adj(g).wait()
        products = []
        for i in range(GROUP):
            s = g * GROUP + i
            products.append(
                jnp.dot(adj_v[s], feat_v[coords_ref[1, s]], preferred_element_type=jnp.float32)
            )
        for i in range(GROUP):
            out_ref[coords_ref[0, g * GROUP + i]] += products[i]
        return carry

    lax.fori_loop(0, turns, turn, 0)


def multiply_blocks(tile_coords, counts, tile_blocks, feature_blocks, row_blocks):
    slots, block, _ = tile_blocks.shape
    width = feature_blocks.shape[-1]
    dma = pltpu.SemaphoreType.DMA
    return pl.pallas_call(
        multiply_kernel,
        out_shape=jax.ShapeDtypeStruct((row_blocks, block, width), jnp.float32),
        in_specs=[pl.BlockSpec(memory_space=pltpu.SMEM)] * 2 + [pl.BlockSpec(memory_space=pl.ANY)] * 2,
        out_specs=pl.BlockSpec(memory_space=pltpu.VMEM),
        scratch_shapes=[
            pltpu.VMEM(tile_blocks.shape, tile_blocks.dtype),
            pltpu.VMEM(feature_blocks.shape, feature_blocks.dtype),
            dma((slots // GROUP,)),
            dma,
        ],
        compiler_params=pltpu.CompilerParams(vmem_limit_bytes=24 << 20),
        name="multiply_blocks",
    )(tile_coords, counts, tile_blocks, feature_blocks)


def silu_slope(preact, sigmoid_value):
    return sigmoid_value * (1.0 + preact * (1.0 - sigmoid_value))


def layer_kernel(
    p_ref, w_ref, cot_ref, act_ref, grad_ref,
    ysend, yrecv, zsend, zrecv, own_ref, rounded_ref, grad_v, r1, c1, r2, c2, r3, c3, r4,
    ys_s, ys_r, zs_s, zs_r, g_s, g_r,
):
    rows = cot_ref.shape[0]
    half = rows // 2
    members = NX * NY * NC
    r, c = lax.axis_index("row"), lax.axis_index("col")
    x, z, core = r // (NZ * NC), (r // NC) % NZ, r % NC
    y, h = c // NH, c % NH
    me = (x * NY + y) * NC + core

    def member(m):
        return {"row": ((m // (NY * NC)) * NZ + z) * NC + m % NC, "col": ((m // NC) % NY) * NH + h}

    def z_peer(zz):
        return {"row": (x * NZ + zz) * NC + core, "col": c}

    def h_peer(hh):
        return {"row": r, "col": y * NH + hh % NH}

    barrier = pltpu.get_barrier_semaphore()

    def greet(j, carry):
        pl.semaphore_signal(barrier, inc=1, device_id=member((me + j) % members), device_id_type=MESH)
        return carry

    lax.fori_loop(1, members, greet, 0)
    for j in range(1, NZ):
        pl.semaphore_signal(barrier, inc=1, device_id=z_peer((z + j) % NZ), device_id_type=MESH)
    for j in range(1, NH):
        pl.semaphore_signal(barrier, inc=1, device_id=h_peer(h + j), device_id_type=MESH)

    def part(dy, k, b):
        start = (((y + dy) % NY) * NH + (h + k) % NH) * rows + b * half
        return p_ref[pl.ds(pl.multiple_of(start, half), half), :]

    def y_copy(k, i):
        yy = (y + (1 if i % 2 == 0 else NY - 1)) % NY
        return remote(
            ysend.at[k, i], yrecv.at[k, i], ys_s.at[k, i], ys_r.at[k, i], {"row": r, "col": yy * NH + h}
        )

    def z_copy(i):
        return remote(
            zsend.at[i], zrecv.at[i], zs_s.at[i], zs_r.at[i], h_peer(h + (1 if i % 2 == 0 else NH - 1))
        )

    def y_fill(k, i):
        s, w = i // 2, i % 2
        dy = 2 if s == 0 else (1 if w == 0 else -1)
        b = w if s != 1 else 1 - w
        value = part(dy, k, b)
        if s == 2:
            value = value + yrecv[k, w].astype(jnp.float32)
        ysend[k, i] = value.astype(ysend.dtype)

    def y_middle(k):
        for w in range(2):
            y_copy(k, w).wait_recv()
            y_fill(k, 4 + w)
            y_copy(k, 4 + w).start()

    def y_sum(k, b):
        first, second = (4, 3) if b == 0 else (2, 5)
        return part(0, k, b) + yrecv[k, first].astype(jnp.float32) + yrecv[k, second].astype(jnp.float32)

    def y_end(k):
        for i in range(2, 6):
            y_copy(k, i).wait_recv()

    def z_start(i, value):
        zsend[i] = value.astype(zsend.dtype)
        z_copy(i).start()

    def y_launch(k):
        for i in range(4):
            y_copy(k, i).start()

    for i in range(4):
        y_fill(2, i)
    pl.semaphore_wait(barrier, members - 1 + NZ - 1 + NH - 1)
    y_launch(2)
    for i in range(4):
        y_fill(1, i)
    y_launch(1)
    for k in (3, 0):
        for i in range(4):
            y_fill(k, i)
    y_middle(2)
    y_launch(3)
    y_middle(1)
    y_end(2)
    z_start(0, y_sum(2, 0))
    z_start(1, y_sum(2, 1))
    y_launch(0)
    y_middle(3)
    y_end(1)
    z_start(2, y_sum(1, 1))
    y_middle(0)
    y_end(3)
    z_start(3, y_sum(3, 0))
    z_copy(0).wait_recv()
    z_start(4, y_sum(1, 0) + zrecv[0].astype(jnp.float32))
    z_copy(1).wait_recv()
    z_start(5, y_sum(3, 1) + zrecv[1].astype(jnp.float32))
    y_end(0)
    own_ref[0] = y_sum(0, 0)
    own_ref[1] = y_sum(0, 1)
    z_copy(2).wait_recv()
    z_copy(3).wait_recv()
    z_copy(4).wait_recv()
    z_copy(5).wait_recv()
    for b, (first, second) in enumerate(((4, 3), (2, 5))):
        total = own_ref[b] + zrecv[first].astype(jnp.float32) + zrecv[second].astype(jnp.float32)
        rounded_ref[pl.ds(b * half, half), :] = total.astype(rounded_ref.dtype)

    rounded = rounded_ref[...]
    preact = jnp.dot(rounded, w_ref[...], preferred_element_type=jnp.float32)
    sigmoid_value = 1.0 / (1.0 + jnp.exp(-preact))
    act_ref[...] = (preact * sigmoid_value).astype(act_ref.dtype)
    slope_grad = (cot_ref[...].astype(jnp.float32) * silu_slope(preact, sigmoid_value)).astype(jnp.bfloat16)
    local_grad = lax.dot_general(
        rounded, slope_grad, (((0,), (0,)), ((), ())), preferred_element_type=jnp.float32
    )
    lanes = grad_v.shape[-1]
    pieces = local_grad.shape[1] // lanes
    per = members // pieces
    for i in range(pieces):
        grad_v[i * per : (i + 1) * per] = local_grad[:, i * lanes : (i + 1) * lanes].reshape(
            (per,) + grad_v.shape[1:]
        )

    def scatter(j, carry):
        m = (me + j) % members
        remote(grad_v.at[m], r1.at[j - 1], g_s.at[0], g_r.at[0], member(m)).start()
        return carry

    lax.fori_loop(1, members, scatter, 0)
    remote(r1, r1, g_s.at[0], g_r.at[0], member(me)).wait_recv()
    c1[...] = grad_v[me] + jnp.sum(r1[...], axis=0)
    for j in range(1, NZ):
        remote(c1, r2.at[z], g_s.at[1], g_r.at[1], z_peer((z + j) % NZ)).start()
    r2[z] = c1[...]
    remote(r1.at[: NZ - 1], r1.at[: NZ - 1], g_s.at[1], g_r.at[1], member(me)).wait_recv()
    c2[...] = jnp.sum(r2[...], axis=0)
    for j in range(1, NH):
        remote(c2, r3.at[h], g_s.at[2], g_r.at[2], h_peer(h + j)).start()
    r3[h] = c2[...]
    remote(r1.at[: NH - 1], r1.at[: NH - 1], g_s.at[2], g_r.at[2], member(me)).wait_recv()
    c3[...] = jnp.sum(r3[...], axis=0)

    def hand_out(j, carry):
        remote(c3, r4.at[me], g_s.at[3], g_r.at[3], member((me + j) % members)).start()
        return carry

    lax.fori_loop(1, members, hand_out, 0)
    r4[me] = c3[...]
    for k in range(NH):
        for i in range(6):
            y_copy(k, i).wait_send()
    for i in range(6):
        z_copy(i).wait_send()
    remote(r1, r1, g_s.at[0], g_r.at[0], member(me)).wait_send()
    remote(r1.at[: NZ - 1], r1.at[: NZ - 1], g_s.at[1], g_r.at[1], member(me)).wait_send()
    remote(r1.at[: NH - 1], r1.at[: NH - 1], g_s.at[2], g_r.at[2], member(me)).wait_send()
    remote(r1, r1, g_s.at[3], g_r.at[3], member(me)).wait_recv()
    remote(r1, r1, g_s.at[3], g_r.at[3], member(me)).wait_send()
    for i in range(pieces):
        grad_ref[:, i * lanes : (i + 1) * lanes] = r4[i * per : (i + 1) * per].reshape(grad_ref.shape[0], lanes)


def layer(partial_rows, weight, cotangent):
    rows, hidden = cotangent.shape
    width = weight.shape[0]
    half = rows // 2
    members = NX * NY * NC
    lanes = 128
    chunk = (width * hidden // members // lanes, lanes)
    dma = pltpu.SemaphoreType.DMA
    f32, bf16 = jnp.float32, jnp.bfloat16
    vmem = pl.BlockSpec(memory_space=pltpu.VMEM)
    return pl.pallas_call(
        layer_kernel,
        out_shape=(
            jax.ShapeDtypeStruct((rows, hidden), bf16),
            jax.ShapeDtypeStruct((width, hidden), f32),
        ),
        in_specs=[vmem] * 3,
        out_specs=(vmem, vmem),
        scratch_shapes=[
            pltpu.VMEM((NH, 6, half, width), bf16),
            pltpu.VMEM((NH, 6, half, width), bf16),
            pltpu.VMEM((6, half, width), bf16),
            pltpu.VMEM((6, half, width), bf16),
            pltpu.VMEM((2, half, width), f32),
            pltpu.VMEM((rows, width), bf16),
            pltpu.VMEM((members,) + chunk, f32),
            pltpu.VMEM((members - 1,) + chunk, f32),
            pltpu.VMEM(chunk, f32),
            pltpu.VMEM((NZ,) + chunk, f32),
            pltpu.VMEM(chunk, f32),
            pltpu.VMEM((NH,) + chunk, f32),
            pltpu.VMEM(chunk, f32),
            pltpu.VMEM((members,) + chunk, f32),
            dma((NH, 6)),
            dma((NH, 6)),
            dma((6,)),
            dma((6,)),
            dma((4,)),
            dma((4,)),
        ],
        compiler_params=pltpu.CompilerParams(
            collective_id=1, has_side_effects=True, vmem_limit_bytes=24 << 20
        ),
        name="layer",
    )(partial_rows, weight, cotangent)


def body(features, adj_blocks, block_coords, counts, weight, cotangent):
    tile_blocks, tile_coords = adj_blocks[0, 0], block_coords[0, 0]
    block, width = tile_blocks.shape[1], features.shape[1]
    gathered = gather_features(features)
    feature_blocks = gathered.reshape(-1, block, width)
    row_blocks = cotangent.shape[0] * NY * NH // block
    partial_rows = multiply_blocks(tile_coords, counts, tile_blocks, feature_blocks, row_blocks)
    return layer(partial_rows.reshape(row_blocks * block, width), weight, cotangent)


def solution(mesh):
    return jax.shard_map(
        body,
        mesh=mesh,
        in_specs=(
            P(("col", "row"), None),
            P("row", "col", None, None, None),
            P("row", "col", None, None),
            P(),
            P(),
            P(("row", "col"), None),
        ),
        out_specs=(P(("row", "col"), None), P()),
        check_vma=False,
    )
```

time: 1240 us -> 138 us (0.11)
  waiting for transfers between devices: 1210 us -> 0 us
  Pallas kernels: 0 us -> 133 us
  between operations: 14.4 us -> 0.7 us
    psum x1 -> x0, waiting for transfers between devices: 846 us -> none  [body(): weight_grad = lax.psum(local_grad, ('row', 'col'))]
    reduce_scatter x1 -> x0, waiting for transfers between devices: 221 us -> none  [body(): lax.psum_scatter(partial_rows, 'col', scatter_dimension=0, tiled=True)]
    all_gather x1 -> x0, waiting for transfers between devices: 142 us -> none  [body(): gathered = lax.all_gather(features, 'row', axis=0, tiled=True)]
    pallas_call x0 -> x3, Pallas kernels: none -> 133 us  [the longest x1 77.8 us: layer(): pl.pallas_call(layer_kernel, out_shape=(jax.ShapeDtypeStruct((rows, hidde...]
  transfers between devices with their start and end apart: 3 -> 0, of which waited for: 3 -> 0; matrix products, arithmetic and copies ran while one was open for 0% -> 0% of each run, Pallas kernels for 0% -> 0%
where the time goes in v1:
time: 138 us
  Pallas kernels  133 us (96%)
  local copies, waits for them, and re-layouts  4.29 us (3%)
    pallas_call x1, Pallas kernels, layer(): pl.pallas_call(layer_kernel, out_shape=(jax.ShapeDtypeStruct((rows, hidde...  77.8 us
    pallas_call x1, Pallas kernels, gather_features(): pl.pallas_call(gather_kernel, out_shape=jax.ShapeDtypeStruct((devices, ro...  51.8 us
    unnamed x13, local copies, waits for them, and re-layouts  4.29 us
    pallas_call x1, Pallas kernels, multiply_blocks(): pl.pallas_call(multiply_kernel, out_shape=jax.ShapeDtypeStruct((row_block...  3.11 us

profile of v1, /device:TPU:1, one launch (start us, length us, event | category | flops | bytes accessed | tf_op | source)
XLA Modules:
  0.0 137.7 jit_solution(3283814494995227221)
XLA Ops:
  0.6 0.8 copy.8.counts_ref
  1.4 0.0 copy-start.1
  1.4 0.0 copy-start.4
  1.4 51.8 %gather_features.1 = bf16[64,256,128]{2,1,0:T(8,128)(2,1)} custom-call(bf16[256,128]{1,0:T(8,128)(2,1)} %f_ref.1), custom_call_target="tpu_custom_call" | custom-call | tf_op jit(solution)/shard_map/gather_features/pallas_call | solution.py:183
  53.3 0.0 copy-done.1
  53.3 0.0 copy-done.4
  53.3 0.0 copy-start
  53.3 2.2 %copy-done = bf16[64,256,128]{2,1,0:T(8,128)(2,1)S(1)} copy-done((bf16[64,256,128]{2,1,0:T(8,128)(2,1)S(1)}, bf16[64,256,128]{2,1,0:T(8,128)(2,1)}, u32[]{:S(2)}) %copy-start) | copy-done | bytes 4194328
  55.5 0.0 copy-start.2
  55.5 0.0 copy-start.3
  55.5 3.1 %multiply_blocks.1 = f32[32,128,128]{2,1,0:T(8,128)S(1)} custom-call(s32[2,64]{1,0:T(2,128)S(1)} %bitcast.7, s32[64,16]{1,0:T(8,128)S(1)} %copy.8.counts_ref, bf16[64,128,128]{2,1,0:T(8,128)(2,1)S(1)} %bitcast.6, bf16[128,128,128]{2,1,0:T(8,128)(2,1)S(1)} %bitcast.4), custom_call_target="tpu_custom_call" | custom-call | tf_op jit(solution)/shard_map/multiply_blocks/pallas_call | solution.py:233
  58.6 0.0 copy-done.2
  58.6 0.0 copy-done.3
  58.6 77.8 %layer.1 = (bf16[256,256]{1,0:T(8,128)(2,1)S(1)}, f32[128,256]{1,0:T(8,128)S(1)}) custom-call(f32[4096,128]{1,0:T(8,128)S(1)} %bitcast.5, bf16[128,256]{1,0:T(8,128)(2,1)S(1)} %copy-done.3, bf16[256,256]{1,0:T(8,128)(2,1)S(1)} %copy-done.2), custom_call_target="tpu_custom_call" | custom-call | tf_op jit(solution)/shard_map/layer/pallas_call | solution.py:436
  136.4 0.7 copy.11
  137.0 0.7 copy.12
Async XLA Ops:
  1.4 51.9 %copy-start.1 = (bf16[1,1,64,128,128]{4,3,2,1,0:T(8,128)(2,1)S(1)}, bf16[1,1,64,128,128]{4,3,2,1,0:T(8,128)(2,1)}, u32[]{:S(2)}) copy-start(bf16[1,1,64,128,128]{4,3,2,1,0:T(8,128)(2,1)} %param.7) | copy-start | bytes 6291460
  1.4 51.9 %copy-start.4 = (s32[1,1,2,64]{3,2,1,0:T(2,128)S(1)}, s32[1,1,2,64]{3,2,1,0:T(2,128)}, u32[]{:S(2)}) copy-start(s32[1,1,2,64]{3,2,1,0:T(2,128)} %param.8) | copy-start | bytes 1540
  53.3 2.2 %copy-start = (bf16[64,256,128]{2,1,0:T(8,128)(2,1)S(1)}, bf16[64,256,128]{2,1,0:T(8,128)(2,1)}, u32[]{:S(2)}) copy-start(bf16[64,256,128]{2,1,0:T(8,128)(2,1)} %gather_features.1) | copy-start | bytes 12582916
  55.5 3.1 %copy-start.2 = (bf16[256,256]{1,0:T(8,128)(2,1)S(1)}, bf16[256,256]{1,0:T(8,128)(2,1)}, u32[]{:S(2)}) copy-start(bf16[256,256]{1,0:T(8,128)(2,1)} %cot_ref.1) | copy-start | bytes 393220
  55.5 3.1 %copy-start.3 = (bf16[128,256]{1,0:T(8,128)(2,1)S(1)}, bf16[128,256]{1,0:T(8,128)(2,1)}, u32[]{:S(2)}) copy-start(bf16[128,256]{1,0:T(8,128)(2,1)} %w_ref.1) | copy-start | bytes 196612

commit v2 on v1

v2 whole, which is shorter than its diff:
```python
import jax
import jax.numpy as jnp
from jax import lax
from jax.experimental import pallas as pl
from jax.experimental.pallas import tpu as pltpu
from jax.sharding import PartitionSpec as P

NX, NZ, NC = 4, 8, 2
NY, NH = 4, 4
UNROLL = 4
NEAR = 4
LAG = 2
MESH = pl.DeviceIdType.MESH


def remote(src, dst, send_sem, recv_sem, device):
    return pltpu.make_async_remote_copy(
        src_ref=src, dst_ref=dst, send_sem=send_sem, recv_sem=recv_sem, device_id=device, device_id_type=MESH
    )


def find_links(coords_ref, live, plan_ref):
    slots = coords_ref.shape[1]
    wide = plan_ref.shape[1]
    rows = jnp.broadcast_to(coords_ref[0:1, :], (slots, slots))
    down = lax.broadcasted_iota(jnp.int32, (slots, slots), 0)
    across = lax.broadcasted_iota(jnp.int32, (slots, slots), 1)
    row_of = jnp.sum(jnp.where(down == across, rows, 0), axis=1, keepdims=True)
    earlier = jnp.logical_and(row_of == rows, down < across)
    before = jnp.max(jnp.where(earlier, down, -1), axis=0, keepdims=True)
    plan_ref[...] = jnp.full(plan_ref.shape, slots, jnp.int32)
    plan_ref[0:1, 0:slots] = jnp.where(before < 0, slots, before)
    place = lax.broadcasted_iota(jnp.int32, (slots, wide), 1)
    slot = lax.broadcasted_iota(jnp.int32, (slots, wide), 0)
    named = jnp.logical_and(row_of == place, slot < live)
    last = jnp.max(jnp.where(named, slot, -1), axis=0, keepdims=True)
    plan_ref[1:2, :] = jnp.where(last < 0, slots, last)


def gather_kernel(
    f_ref, coords_ref, counts_ref, out_ref, plan_ref,
    own_sem, zu_s, zu_r, zd_s, zd_r, xs_s, xs_r, xf_s, xf_r, cc_s, cc_r,
):
    half = f_ref.shape[0] // 2
    r = lax.axis_index("row")
    x, z, core = r // (NZ * NC), (r // NC) % NZ, r % NC

    def slot(xx, zz, cc=None):
        return ((xx % NX) * NZ + zz) * NC + (core if cc is None else cc)

    up, down = {"row": slot(x, z + 1)}, {"row": slot(x, z - 1)}
    right, left = {"row": slot(x + 1, z)}, {"row": slot(x - 1, z)}
    other = {"row": slot(x, z, 1 - core)}

    def send(s, b, send_sem, recv_sem, device, src=None):
        rows = pl.ds(b * half, half)
        there = out_ref.at[s, rows]
        return remote(there if src is None else src.at[rows], there, send_sem, recv_sem, device)

    def z_up(d, b, src=None):
        return send(slot(x, z - d), b, zu_s.at[d, b], zu_r.at[d, b], up, src)

    def z_down(d, b, src=None):
        return send(slot(x, z + d), b, zd_s.at[d, b], zd_r.at[d, b], down, src)

    def z_up_arrival(d, b):
        return send(slot(x, z - d), b, zu_s.at[d - 1, b], zu_r.at[d - 1, b], up)

    def z_down_arrival(d, b):
        return send(slot(x, z + d), b, zd_s.at[d - 1, b], zd_r.at[d - 1, b], down)

    def x_copy(zz, way, b, src=None):
        return send(
            slot(x, zz), b, xs_s.at[way, zz, b], xs_r.at[way, zz, b], right if way == 0 else left, src
        )

    def x_arrival(zz, way, b):
        s = slot(x - 1 if way == 0 else x + 1, zz)
        return send(s, b, xs_s.at[way, zz, b], xs_r.at[way, zz, b], right)

    def x_forward(zz, way):
        s = slot(x - 1 if way == 0 else x + 1, zz)
        return send(s, way, xf_s.at[way, zz], xf_r.at[way, zz], right if way == 0 else left)

    def f_arrival(zz, way):
        return send(slot(x + 2, zz), way, xf_s.at[way, zz], xf_r.at[way, zz], right)

    def cross(dx, zz, src=None):
        there = out_ref.at[slot(x + dx, zz)]
        return remote(there if src is None else src, there, cc_s.at[dx, zz], cc_r.at[dx, zz], other)

    def cross_arrival(dx, zz):
        here = out_ref.at[slot(x + dx, zz, 1 - core)]
        return remote(here, here, cc_s.at[dx, zz], cc_r.at[dx, zz], other)

    has_up, has_down = z < NZ - 1, z > 0
    barrier = pltpu.get_barrier_semaphore()
    for device in (right, left, other):
        pl.semaphore_signal(barrier, inc=1, device_id=device, device_id_type=MESH)

    @pl.when(has_up)
    def _():
        pl.semaphore_signal(barrier, inc=1, device_id=up, device_id_type=MESH)

    @pl.when(has_down)
    def _():
        pl.semaphore_signal(barrier, inc=1, device_id=down, device_id_type=MESH)

    own = pltpu.make_async_copy(f_ref, out_ref.at[r], own_sem)
    own.start()
    pl.semaphore_wait(barrier, 3 + has_up.astype(jnp.int32) + has_down.astype(jnp.int32))

    for b in range(2):
        pl.when(has_up)(lambda b=b: z_up(0, b, f_ref).start())
        pl.when(has_down)(lambda b=b: z_down(0, b, f_ref).start())
        x_copy(z, 0, b, f_ref).start()
        x_copy(z, 1, 1 - b, f_ref).start()
    cross(0, z, f_ref).start()
    find_links(coords_ref, counts_ref[r, lax.axis_index("col")], plan_ref)

    def along_z(d):
        below, above = z - d >= 0, z + d < NZ
        for b in range(2):

            @pl.when(below)
            def _():
                z_up_arrival(d, b).wait_recv()
                pl.when(has_up)(lambda: z_up(d, b).start())
                x_copy(z - d, 0, b).start()
                x_copy(z - d, 1, b).start()

            @pl.when(above)
            def _():
                z_down_arrival(d, b).wait_recv()
                pl.when(has_down)(lambda: z_down(d, b).start())
                x_copy(z + d, 0, b).start()
                x_copy(z + d, 1, b).start()

        pl.when(below)(lambda: cross(0, z - d).start())
        pl.when(above)(lambda: cross(0, z + d).start())

    def along_x(zz):
        for way in range(2):
            x_arrival(zz, way, way).wait_recv()
            x_forward(zz, way).start()
        x_arrival(zz, 0, 1).wait_recv()
        cross(NX - 1, zz).start()
        x_arrival(zz, 1, 0).wait_recv()
        cross(1, zz).start()

    def last_halves(zz):
        f_arrival(zz, 0).wait_recv()
        f_arrival(zz, 1).wait_recv()
        cross(2, zz).start()

    def at_distance(d, act):
        pl.when(z - d >= 0)(lambda: act(z - d))
        pl.when(jnp.logical_and(d > 0, z + d < NZ))(lambda: act(z + d))

    def first_steps(d, carry):
        along_z(d)
        return carry

    def steps(d, carry):
        along_z(d)
        at_distance(d - LAG, along_x)
        return carry

    def last_x(d, carry):
        at_distance(d, along_x)
        return carry

    def last_steps(d, carry):
        at_distance(d, last_halves)
        return carry

    lax.fori_loop(1, LAG, first_steps, 0)
    lax.fori_loop(LAG, NZ, steps, 0)
    lax.fori_loop(NZ - LAG, NZ, last_x, 0)
    lax.fori_loop(0, NZ, last_steps, 0)

    def drain(zz, carry):
        for dx in range(NX):
            cross_arrival(dx, zz).wait_recv()
            cross(dx, zz).wait_send()
        for way in range(2):
            x_forward(zz, way).wait_send()
        for b in range(2):
            x_copy(zz, 0, b).wait_send()
            x_copy(zz, 1, b).wait_send()
            pl.when(jnp.logical_and(has_up, zz <= z))(lambda b=b: z_up(zz, b).wait_send())
            pl.when(jnp.logical_and(has_down, zz <= NZ - 1 - z))(lambda b=b: z_down(zz, b).wait_send())
        return carry

    lax.fori_loop(0, NZ, drain, 0)
    own.wait()


def gather_features(features, tile_coords, counts):
    rows, width = features.shape
    devices = NX * NZ * NC
    dma = pltpu.SemaphoreType.DMA
    vmem = pl.BlockSpec(memory_space=pltpu.VMEM)
    return pl.pallas_call(
        gather_kernel,
        out_shape=(
            jax.ShapeDtypeStruct((devices, rows, width), features.dtype),
            jax.ShapeDtypeStruct((2, 128), jnp.int32),
        ),
        in_specs=[pl.BlockSpec(memory_space=pl.ANY), vmem, pl.BlockSpec(memory_space=pltpu.SMEM)],
        out_specs=(pl.BlockSpec(memory_space=pl.ANY), vmem),
        scratch_shapes=[dma]
        + [dma((NZ, 2))] * 4
        + [dma((2, NZ, 2))] * 2
        + [dma((2, NZ))] * 2
        + [dma((NX, NZ))] * 2,
        compiler_params=pltpu.CompilerParams(
            collective_id=0, has_side_effects=True, vmem_limit_bytes=48 << 20
        ),
        name="gather_features",
    )(features, tile_coords, counts)


def silu_slope(preact, sigmoid_value):
    return sigmoid_value * (1.0 + preact * (1.0 - sigmoid_value))


def layer_kernel(
    cols_ref, plan_ref, adj_ref, feat_ref, w_ref, cot_ref, act_ref, grad_ref,
    adj_v, feat_v, sums, ysend, yrecv, zsend, zrecv, own_ref, rounded_ref, grad_v, r1, c1, r2, c2, r3, c3, r4,
    in_sem, ys_s, ys_r, zs_s, zs_r, g_s, g_r,
):
    rows = cot_ref.shape[0]
    half = rows // 2
    members = NX * NY * NC
    r, c = lax.axis_index("row"), lax.axis_index("col")
    x, z, core = r // (NZ * NC), (r // NC) % NZ, r % NC
    y, h = c // NH, c % NH
    me = (x * NY + y) * NC + core
    tall = NZ * NH
    far = tall // NEAR
    level = h * NZ + z
    place, team = level % NEAR, level // NEAR
    slots = adj_ref.shape[0]

    adj = pltpu.make_async_copy(adj_ref, adj_v, in_sem.at[0])
    feat = pltpu.make_async_copy(feat_ref, feat_v, in_sem.at[1])
    feat.start()
    adj.start()

    def member(m):
        return {"row": ((m // (NY * NC)) * NZ + z) * NC + m % NC, "col": ((m // NC) % NY) * NH + h}

    def at_level(t):
        return {"row": (x * NZ + t % NZ) * NC + core, "col": y * NH + t // NZ}

    def near_peer(j):
        return at_level(team * NEAR + (place + j) % NEAR)

    def far_peer(j):
        return at_level((level + j * NEAR) % tall)

    def h_peer(hh):
        return {"row": r, "col": y * NH + hh % NH}

    barrier = pltpu.get_barrier_semaphore()

    def greet(j, carry):
        pl.semaphore_signal(barrier, inc=1, device_id=member((me + j) % members), device_id_type=MESH)
        return carry

    lax.fori_loop(1, members, greet, 0)
    for j in range(1, NEAR):
        pl.semaphore_signal(barrier, inc=1, device_id=near_peer(j), device_id_type=MESH)
    for j in range(1, far):
        pl.semaphore_signal(barrier, inc=1, device_id=far_peer(j), device_id_type=MESH)

    sums[slots] = jnp.zeros(sums.shape[1:], sums.dtype)
    feat.wait()
    adj.wait()

    def turn(g, carry):
        first = g * UNROLL
        products = [
            jnp.dot(adj_v[first + i], feat_v[cols_ref[0, first + i]], preferred_element_type=jnp.float32)
            for i in range(UNROLL)
        ]
        for i in range(UNROLL):
            sums[first + i] = products[i] + sums[plan_ref[0, first + i]]
        return carry

    lax.fori_loop(0, slots // UNROLL, turn, 0)

    def part(dy, k, b):
        block_row = (((y + dy) % NY) * NH + (h + k) % NH) * 2 + b
        return sums[plan_ref[1, block_row]]

    def y_copy(k, i):
        yy = (y + (1 if i % 2 == 0 else NY - 1)) % NY
        return remote(
            ysend.at[k, i], yrecv.at[k, i], ys_s.at[k, i], ys_r.at[k, i], {"row": r, "col": yy * NH + h}
        )

    def z_copy(i):
        return remote(
            zsend.at[i], zrecv.at[i], zs_s.at[i], zs_r.at[i], h_peer(h + (1 if i % 2 == 0 else NH - 1))
        )

    def y_fill(k, i):
        s, w = i // 2, i % 2
        dy = 2 if s == 0 else (1 if w == 0 else -1)
        b = w if s != 1 else 1 - w
        value = part(dy, k, b)
        if s == 2:
            value = value + yrecv[k, w].astype(jnp.float32)
        ysend[k, i] = value.astype(ysend.dtype)

    def y_middle(k):
        for w in range(2):
            y_copy(k, w).wait_recv()
            y_fill(k, 4 + w)
            y_copy(k, 4 + w).start()

    def y_sum(k, b):
        first, second = (4, 3) if b == 0 else (2, 5)
        return part(0, k, b) + yrecv[k, first].astype(jnp.float32) + yrecv[k, second].astype(jnp.float32)

    def y_end(k):
        for i in range(2, 6):
            y_copy(k, i).wait_recv()

    def z_start(i, value):
        zsend[i] = value.astype(zsend.dtype)
        z_copy(i).start()

    def y_launch(k):
        for i in range(4):
            y_copy(k, i).start()

    for i in range(4):
        y_fill(2, i)
    pl.semaphore_wait(barrier, members - 1 + NEAR - 1 + far - 1)
    y_launch(2)
    for i in range(4):
        y_fill(1, i)
    y_launch(1)
    for k in (3, 0):
        for i in range(4):
            y_fill(k, i)
    y_middle(2)
    y_launch(3)
    y_middle(1)
    y_end(2)
    z_start(0, y_sum(2, 0))
    z_start(1, y_sum(2, 1))
    y_launch(0)
    y_middle(3)
    y_end(1)
    z_start(2, y_sum(1, 1))
    y_middle(0)
    y_end(3)
    z_start(3, y_sum(3, 0))
    z_copy(0).wait_recv()
    z_start(4, y_sum(1, 0) + zrecv[0].astype(jnp.float32))
    z_copy(1).wait_recv()
    z_start(5, y_sum(3, 1) + zrecv[1].astype(jnp.float32))
    y_end(0)
    own_ref[0] = y_sum(0, 0)
    own_ref[1] = y_sum(0, 1)
    z_copy(2).wait_recv()
    z_copy(3).wait_recv()
    z_copy(4).wait_recv()
    z_copy(5).wait_recv()
    for b, (first, second) in enumerate(((4, 3), (2, 5))):
        total = own_ref[b] + zrecv[first].astype(jnp.float32) + zrecv[second].astype(jnp.float32)
        rounded_ref[pl.ds(b * half, half), :] = total.astype(rounded_ref.dtype)

    rounded = rounded_ref[...]
    preact = jnp.dot(rounded, w_ref[...], preferred_element_type=jnp.float32)
    sigmoid_value = 1.0 / (1.0 + jnp.exp(-preact))
    act_ref[...] = (preact * sigmoid_value).astype(act_ref.dtype)
    slope_grad = (cot_ref[...].astype(jnp.float32) * silu_slope(preact, sigmoid_value)).astype(jnp.bfloat16)
    local_grad = lax.dot_general(
        rounded, slope_grad, (((0,), (0,)), ((), ())), preferred_element_type=jnp.float32
    )
    lanes = grad_v.shape[-1]
    pieces = local_grad.shape[1] // lanes
    per = members // pieces
    for i in range(pieces):
        grad_v[i * per : (i + 1) * per] = local_grad[:, i * lanes : (i + 1) * lanes].reshape(
            (per,) + grad_v.shape[1:]
        )

    def scatter(j, carry):
        m = (me + j) % members
        remote(grad_v.at[m], r1.at[j - 1], g_s.at[0], g_r.at[0], member(m)).start()
        return carry

    lax.fori_loop(1, members, scatter, 0)
    remote(r1, r1, g_s.at[0], g_r.at[0], member(me)).wait_recv()
    c1[...] = grad_v[me] + jnp.sum(r1[...], axis=0)
    for j in range(1, NEAR):
        remote(c1, r2.at[place], g_s.at[1], g_r.at[1], near_peer(j)).start()
    r2[place] = c1[...]
    remote(r1.at[: NEAR - 1], r1.at[: NEAR - 1], g_s.at[1], g_r.at[1], member(me)).wait_recv()
    c2[...] = jnp.sum(r2[...], axis=0)
    for j in range(1, far):
        remote(c2, r3.at[team], g_s.at[2], g_r.at[2], far_peer(far - j)).start()
    r3[team] = c2[...]
    remote(r1.at[: far - 1], r1.at[: far - 1], g_s.at[2], g_r.at[2], member(me)).wait_recv()
    c3[...] = jnp.sum(r3[...], axis=0)

    def hand_out(j, carry):
        remote(c3, r4.at[me], g_s.at[3], g_r.at[3], member((me + j) % members)).start()
        return carry

    lax.fori_loop(1, members, hand_out, 0)
    r4[me] = c3[...]
    for k in range(NH):
        for i in range(6):
            y_copy(k, i).wait_send()
    for i in range(6):
        z_copy(i).wait_send()
    remote(r1, r1, g_s.at[0], g_r.at[0], member(me)).wait_send()
    remote(r1.at[: NEAR - 1], r1.at[: NEAR - 1], g_s.at[1], g_r.at[1], member(me)).wait_send()
    remote(r1.at[: far - 1], r1.at[: far - 1], g_s.at[2], g_r.at[2], member(me)).wait_send()
    remote(r1, r1, g_s.at[3], g_r.at[3], member(me)).wait_recv()
    remote(r1, r1, g_s.at[3], g_r.at[3], member(me)).wait_send()
    for i in range(pieces):
        grad_ref[:, i * lanes : (i + 1) * lanes] = r4[i * per : (i + 1) * per].reshape(grad_ref.shape[0], lanes)


def layer(cols, plan, tile_blocks, feature_blocks, weight, cotangent):
    rows, hidden = cotangent.shape
    width = weight.shape[0]
    half = rows // 2
    members = NX * NY * NC
    lanes = 128
    chunk = (width * hidden // members // lanes, lanes)
    dma = pltpu.SemaphoreType.DMA
    f32, bf16 = jnp.float32, jnp.bfloat16
    vmem = pl.BlockSpec(memory_space=pltpu.VMEM)
    smem, hbm = pl.BlockSpec(memory_space=pltpu.SMEM), pl.BlockSpec(memory_space=pl.ANY)
    slots, block, _ = tile_blocks.shape
    return pl.pallas_call(
        layer_kernel,
        out_shape=(
            jax.ShapeDtypeStruct((rows, hidden), bf16),
            jax.ShapeDtypeStruct((width, hidden), f32),
        ),
        in_specs=[smem, smem, hbm, hbm, vmem, vmem],
        out_specs=(vmem, vmem),
        scratch_shapes=[
            pltpu.VMEM(tile_blocks.shape, bf16),
            pltpu.VMEM(feature_blocks.shape, bf16),
            pltpu.VMEM((slots + 1, block, width), f32),
            pltpu.VMEM((NH, 6, half, width), bf16),
            pltpu.VMEM((NH, 6, half, width), bf16),
            pltpu.VMEM((6, half, width), bf16),
            pltpu.VMEM((6, half, width), bf16),
            pltpu.VMEM((2, half, width), f32),
            pltpu.VMEM((rows, width), bf16),
            pltpu.VMEM((members,) + chunk, f32),
            pltpu.VMEM((members - 1,) + chunk, f32),
            pltpu.VMEM(chunk, f32),
            pltpu.VMEM((NEAR,) + chunk, f32),
            pltpu.VMEM(chunk, f32),
            pltpu.VMEM((NZ * NH // NEAR,) + chunk, f32),
            pltpu.VMEM(chunk, f32),
            pltpu.VMEM((members,) + chunk, f32),
            dma((2,)),
            dma((NH, 6)),
            dma((NH, 6)),
            dma((6,)),
            dma((6,)),
            dma((4,)),
            dma((4,)),
        ],
        compiler_params=pltpu.CompilerParams(
            collective_id=1, has_side_effects=True, vmem_limit_bytes=48 << 20
        ),
        name="layer",
    )(cols, plan, tile_blocks, feature_blocks, weight, cotangent)


def body(features, adj_blocks, block_coords, counts, weight, cotangent):
    tile_blocks, tile_coords = adj_blocks[0, 0], block_coords[0, 0]
    block, width = tile_blocks.shape[1], features.shape[1]
    gathered, plan = gather_features(features, tile_coords, counts)
    feature_blocks = gathered.reshape(-1, block, width)
    return layer(tile_coords[1:], plan, tile_blocks, feature_blocks, weight, cotangent)


def solution(mesh):
    return jax.shard_map(
        body,
        mesh=mesh,
        in_specs=(
            P(("col", "row"), None),
            P("row", "col", None, None, None),
            P("row", "col", None, None),
            P(),
            P(),
            P(("row", "col"), None),
        ),
        out_specs=(P(("row", "col"), None), P()),
        check_vma=False,
    )
```

time: 138 us -> 133 us (0.964)
  Pallas kernels: 133 us -> 123 us
  local copies, waits for them, and re-layouts: 4.29 us -> 9.56 us
    pallas_call x2 -> x1, Pallas kernels: 54.9 us -> 47.4 us  [gather_features(): pl.pallas_call(gather_kernel, out_shape=(jax.ShapeDtypeStruct((devices, r...]
    unnamed x13 -> x15, local copies, waits for them, and re-layouts: 4.29 us -> 8.88 us
    pallas_call x1, Pallas kernels: 77.8 us -> 75.2 us  [layer(): pl.pallas_call(layer_kernel, out_shape=(jax.ShapeDtypeStruct((rows, hidde...]
where the time goes in v2:
time: 133 us
  Pallas kernels  123 us (92%)
  local copies, waits for them, and re-layouts  9.56 us (7%)
    pallas_call x1, Pallas kernels, layer(): pl.pallas_call(layer_kernel, out_shape=(jax.ShapeDtypeStruct((rows, hidde...  75.2 us
    pallas_call x1, Pallas kernels, gather_features(): pl.pallas_call(gather_kernel, out_shape=(jax.ShapeDtypeStruct((devices, r...  47.4 us
    unnamed x15, local copies, waits for them, and re-layouts  8.88 us

profile of v2, /device:TPU:1, one launch (start us, length us, event | category | flops | bytes accessed | tf_op | source)
XLA Modules:
  0.0 132.9 jit_solution(8450439273195496043)
XLA Ops:
  0.6 0.7 slice_bitcast_fusion.cols_ref
  1.3 0.8 copy.8.counts_ref
  2.1 0.0 copy-start.4
  2.1 0.8 copy-done.4
  2.9 0.0 copy-start.5
  2.9 0.7 copy-done.5
  3.6 47.4 %gather_features.1 = (bf16[64,256,128]{2,1,0:T(8,128)(2,1)S(1)}, s32[2,128]{1,0:T(2,128)S(1)}) custom-call(bf16[256,128]{1,0:T(8,128)(2,1)S(1)} %copy-done.4, s32[2,64]{1,0:T(2,128)S(1)} %bitcast.7, s32[64,16]{1,0:T(8,128)S(1)} %copy.8.counts_ref), custom_call_target="tpu_custom_call" | custom-call | tf_op jit(solution)/shard_map/gather_features/pallas_call | solution.py:204
  51.1 0.0 copy-start
  51.1 1.9 %copy-done = bf16[64,256,128]{2,1,0:T(8,128)(2,1)} copy-done((bf16[64,256,128]{2,1,0:T(8,128)(2,1)}, bf16[64,256,128]{2,1,0:T(8,128)(2,1)S(1)}, u32[]{:S(2)}) %copy-start) | copy-done | bytes 4194328
  53.0 0.0 copy-start.1
  53.0 1.6 %copy-done.1 = bf16[1,1,64,128,128]{4,3,2,1,0:T(8,128)(2,1)S(1)} copy-done((bf16[1,1,64,128,128]{4,3,2,1,0:T(8,128)(2,1)S(1)}, bf16[1,1,64,128,128]{4,3,2,1,0:T(8,128)(2,1)}, u32[]{:S(2)}) %copy-start.1) | copy-done | bytes 2097176
  54.6 0.0 copy-start.2
  54.6 0.9 copy-done.2
  55.5 0.0 copy-start.3
  55.5 0.8 copy-done.3
  56.3 75.2 %layer.1 = (bf16[256,256]{1,0:T(8,128)(2,1)S(1)}, f32[128,256]{1,0:T(8,128)S(1)}) custom-call(s32[1,64]{1,0:T(1,128)S(1)} %slice_bitcast_fusion.cols_ref, s32[2,128]{1,0:T(2,128)S(1)} %get-tuple-element.4.plan_ref, bf16[64,128,128]{2,1,0:T(8,128)(2,1)S(1)} %bitcast.6, bf16[128,128,128]{2,1,0:T(8,128)(2,1)} %bitcast.5, bf16[128,256]{1,0:T(8,128)(2,1)S(1)} %copy-done.3, ...), custom_call_target="tpu_custom_call" | custom-call | tf_op jit(solution)/shard_map/layer/pallas_call | solution.py:445
  131.5 0.7 copy.11
  132.2 0.7 copy.12
Async XLA Ops:
  2.1 0.8 copy-start.4
  2.9 0.7 copy-start.5
  51.1 1.9 %copy-start = (bf16[64,256,128]{2,1,0:T(8,128)(2,1)}, bf16[64,256,128]{2,1,0:T(8,128)(2,1)S(1)}, u32[]{:S(2)}) copy-start(bf16[64,256,128]{2,1,0:T(8,128)(2,1)S(1)} %get-tuple-element.5) | copy-start | bytes 12582916
  53.0 1.6 %copy-start.1 = (bf16[1,1,64,128,128]{4,3,2,1,0:T(8,128)(2,1)S(1)}, bf16[1,1,64,128,128]{4,3,2,1,0:T(8,128)(2,1)}, u32[]{:S(2)}) copy-start(bf16[1,1,64,128,128]{4,3,2,1,0:T(8,128)(2,1)} %param.7) | copy-start | bytes 6291460
  54.6 0.9 copy-start.2
  55.5 0.8 copy-start.3

commit v3 on v0

v3 whole, which is shorter than its diff:
```python
import jax
import jax.numpy as jnp
from jax import lax
from jax.experimental import pallas as pl
from jax.experimental.pallas import tpu as pltpu
from jax.sharding import PartitionSpec as P

NX, NZ, NC = 4, 8, 2
NY, NH = 4, 4
NEAR = 4
UNROLL = 8
MESH = pl.DeviceIdType.MESH
F32, BF16 = jnp.float32, jnp.bfloat16


def remote(src, dst, send_sem, recv_sem, device):
    return pltpu.make_async_remote_copy(
        src_ref=src, dst_ref=dst, send_sem=send_sem, recv_sem=recv_sem, device_id=device, device_id_type=MESH
    )


class Place:
    def __init__(self):
        self.r, self.c = lax.axis_index("row"), lax.axis_index("col")
        self.x, self.z, self.core = self.r // (NZ * NC), (self.r // NC) % NZ, self.r % NC
        self.y, self.h = self.c // NH, self.c % NH
        self.members = NX * NY * NC
        self.me = (self.x * NY + self.y) * NC + self.core
        self.tall = NZ * NH
        self.level = self.h * NZ + self.z
        self.near, self.team = self.level % NEAR, self.level // NEAR

    def slot(self, x, z, core=None):
        return ((x % NX) * NZ + z) * NC + (self.core if core is None else core)

    def in_column(self, x, z, core=None):
        return {"row": self.slot(x, z, core), "col": self.c}

    def member(self, m):
        return {
            "row": ((m // (NY * NC)) * NZ + self.z) * NC + m % NC,
            "col": ((m // NC) % NY) * NH + self.h,
        }

    def at_level(self, t):
        return {"row": (self.x * NZ + t % NZ) * NC + self.core, "col": self.y * NH + t // NZ}

    def up(self, steps):
        return self.at_level((self.level + steps) % self.tall)

    def at_y(self, y):
        return {"row": self.r, "col": (y % NY) * NH + self.h}

    def at_h(self, h):
        return {"row": self.r, "col": self.y * NH + h % NH}

    def offsets(self, steps):
        return sorted({s % self.tall for s in steps} - {0})


def meet(p):
    barrier = pltpu.get_barrier_semaphore()
    near = p.offsets(range(-NEAR, NEAR + 1))
    for s in near:
        pl.semaphore_signal(barrier, inc=1, device_id=p.up(s), device_id_type=MESH)

    def greet(j, carry):
        pl.semaphore_signal(barrier, inc=1, device_id=p.member((p.me + j) % p.members), device_id_type=MESH)
        return carry

    lax.fori_loop(1, p.members, greet, 0)
    pl.semaphore_wait(barrier, p.members - 1 + len(near))


def tell(p, sem, steps):
    for s in p.offsets((-steps, steps)):
        pl.semaphore_signal(sem, inc=1, device_id=p.up(s), device_id_type=MESH)


def hear(p, sem, steps):
    if p.offsets((-steps, steps)):
        pl.semaphore_wait(sem, len(p.offsets((-steps, steps))))


class Gather:
    def __init__(self, p, f_ref, out_ref, zu_s, zu_r, zd_s, zd_r, xs_s, xs_r, xf_s, xf_r, cc_s, cc_r):
        self.p, self.f_ref, self.out_ref = p, f_ref, out_ref
        self.zu_s, self.zu_r, self.zd_s, self.zd_r = zu_s, zu_r, zd_s, zd_r
        self.xs_s, self.xs_r, self.xf_s, self.xf_r, self.cc_s, self.cc_r = xs_s, xs_r, xf_s, xf_r, cc_s, cc_r
        self.has_up, self.has_down = p.z < NZ - 1, p.z > 0
        self.far_up, self.far_down = p.z + NEAR < NZ, p.z - NEAR >= 0
        self.right, self.left = p.in_column(p.x + 1, p.z), p.in_column(p.x - 1, p.z)
        self.other = p.in_column(p.x, p.z, 1 - p.core)

    def send(self, s, b, send_sem, recv_sem, device, own=False):
        there = self.out_ref.at[2 * s + b]
        return remote(self.f_ref.at[b] if own else there, there, send_sem, recv_sem, device)

    def both(self, s):
        return self.out_ref.at[pl.ds(2 * s, 2)]

    def z_up(self, d, b, own=False, steps=1):
        k = d + steps - 1
        device = self.p.in_column(self.p.x, self.p.z + steps)
        return self.send(self.p.slot(self.p.x, self.p.z - d), b, self.zu_s.at[k, b], self.zu_r.at[k, b], device, own)

    def z_down(self, d, b, own=False, steps=1):
        k = d + steps - 1
        device = self.p.in_column(self.p.x, self.p.z - steps)
        return self.send(self.p.slot(self.p.x, self.p.z + d), b, self.zd_s.at[k, b], self.zd_r.at[k, b], device, own)

    def z_up_arrival(self, d, b):
        s = self.p.slot(self.p.x, self.p.z - d)
        return self.send(s, b, self.zu_s.at[d - 1, b], self.zu_r.at[d - 1, b], self.other)

    def z_down_arrival(self, d, b):
        s = self.p.slot(self.p.x, self.p.z + d)
        return self.send(s, b, self.zd_s.at[d - 1, b], self.zd_r.at[d - 1, b], self.other)

    def x_copy(self, z, way, b, own=False):
        device = self.right if way == 0 else self.left
        return self.send(self.p.slot(self.p.x, z), b, self.xs_s.at[way, z, b], self.xs_r.at[way, z, b], device, own)

    def x_arrival(self, z, way, b):
        s = self.p.slot(self.p.x - 1 if way == 0 else self.p.x + 1, z)
        return self.send(s, b, self.xs_s.at[way, z, b], self.xs_r.at[way, z, b], self.right)

    def x_forward(self, z, way):
        s = self.p.slot(self.p.x - 1 if way == 0 else self.p.x + 1, z)
        device = self.right if way == 0 else self.left
        return self.send(s, way, self.xf_s.at[way, z], self.xf_r.at[way, z], device)

    def f_arrival(self, z, way):
        return self.send(self.p.slot(self.p.x + 2, z), way, self.xf_s.at[way, z], self.xf_r.at[way, z], self.right)

    def cross(self, dx, z, own=False):
        there = self.both(self.p.slot(self.p.x + dx, z))
        return remote(self.f_ref if own else there, there, self.cc_s.at[dx, z], self.cc_r.at[dx, z], self.other)

    def cross_arrival(self, dx, z):
        here = self.both(self.p.slot(self.p.x + dx, z, 1 - self.p.core))
        return remote(here, here, self.cc_s.at[dx, z], self.cc_r.at[dx, z], self.other)

    def begin(self):
        z = self.p.z
        for b in range(2):
            pl.when(self.has_up)(lambda b=b: self.z_up(0, b, True).start())
            pl.when(self.has_down)(lambda b=b: self.z_down(0, b, True).start())
            self.x_copy(z, 0, b, True).start()
            self.x_copy(z, 1, 1 - b, True).start()
            pl.when(self.far_up)(lambda b=b: self.z_up(0, b, True, NEAR).start())
            pl.when(self.far_down)(lambda b=b: self.z_down(0, b, True, NEAR).start())
        self.cross(0, z, True).start()

    def along_z(self, d, use):
        z = self.p.z
        below, above = jnp.logical_and(use, z - d >= 0), jnp.logical_and(use, z + d < NZ)
        on = d != NEAR - 1
        for b in range(2):

            @pl.when(below)
            def _():
                self.z_up_arrival(d, b).wait_recv()
                pl.when(jnp.logical_and(on, self.has_up))(lambda: self.z_up(d, b).start())
                self.x_copy(z - d, 0, b).start()
                self.x_copy(z - d, 1, b).start()

            @pl.when(above)
            def _():
                self.z_down_arrival(d, b).wait_recv()
                pl.when(jnp.logical_and(on, self.has_down))(lambda: self.z_down(d, b).start())
                self.x_copy(z + d, 0, b).start()
                self.x_copy(z + d, 1, b).start()

        pl.when(below)(lambda: self.cross(0, z - d).start())
        pl.when(above)(lambda: self.cross(0, z + d).start())

    def along_x(self, z):
        for way in range(2):
            self.x_arrival(z, way, way).wait_recv()
            self.x_forward(z, way).start()
        self.x_arrival(z, 0, 1).wait_recv()
        self.cross(NX - 1, z).start()
        self.x_arrival(z, 1, 0).wait_recv()
        self.cross(1, z).start()

    def last_halves(self, z):
        self.f_arrival(z, 0).wait_recv()
        self.f_arrival(z, 1).wait_recv()
        self.cross(2, z).start()

    def at_distance(self, d, act, use=True):
        z = self.p.z
        pl.when(jnp.logical_and(use, z - d >= 0))(lambda: act(z - d))
        pl.when(jnp.logical_and(use, jnp.logical_and(d > 0, z + d < NZ)))(lambda: act(z + d))

    def go_on(self, first, end):
        def distance(k):
            return k // 2 + 1 + (NEAR - 1) * (k % 2)

        def step(k, carry):
            self.along_z(distance(k), k != NZ - 2)
            pl.when(k == 1)(lambda: self.along_x(self.p.z))
            self.at_distance(distance(k - 2), self.along_x, k >= 2)
            return carry

        lax.fori_loop(first, end, step, 0)

    def finish(self):
        self.at_distance(NZ - 1, self.along_x)

        def last(d, carry):
            self.at_distance(d, self.last_halves)
            return carry

        lax.fori_loop(0, NZ, last, 0)

        def arrivals(z, carry):
            for dx in range(NX):
                self.cross_arrival(dx, z).wait_recv()
            return carry

        lax.fori_loop(0, NZ, arrivals, 0)

    def drain(self):
        z = self.p.z

        def sent(k, carry):
            for dx in range(NX):
                self.cross(dx, k).wait_send()
            for way in range(2):
                self.x_forward(k, way).wait_send()
                for b in range(2):
                    self.x_copy(k, way, b).wait_send()
            on = jnp.logical_and(k != NEAR - 1, jnp.logical_and(self.has_up, k <= z))
            back = jnp.logical_and(k != NEAR - 1, jnp.logical_and(self.has_down, k <= NZ - 1 - z))
            for b in range(2):
                pl.when(on)(lambda b=b: self.z_up(k, b).wait_send())
                pl.when(back)(lambda b=b: self.z_down(k, b).wait_send())
            return carry

        lax.fori_loop(0, NZ, sent, 0)
        for b in range(2):
            pl.when(self.far_up)(lambda b=b: self.z_up(0, b, True, NEAR).wait_send())
            pl.when(self.far_down)(lambda b=b: self.z_down(0, b, True, NEAR).wait_send())


def find_links(coords, live, plan_ref):
    slots, wide = coords.shape[1], plan_ref.shape[1]
    rows = jnp.broadcast_to(coords[0:1, :], (slots, slots))
    down = lax.broadcasted_iota(jnp.int32, (slots, slots), 0)
    across = lax.broadcasted_iota(jnp.int32, (slots, slots), 1)
    row_of = jnp.sum(jnp.where(down == across, rows, 0), axis=1, keepdims=True)
    earlier = jnp.logical_and(row_of == rows, down < across)
    before = jnp.max(jnp.where(earlier, down, -1), axis=0, keepdims=True)
    plan_ref[...] = jnp.full(plan_ref.shape, slots, jnp.int32)
    plan_ref[0:1, 0:slots] = jnp.where(before < 0, slots, before)
    place = lax.broadcasted_iota(jnp.int32, (slots, wide), 1)
    slot = lax.broadcasted_iota(jnp.int32, (slots, wide), 0)
    named = jnp.logical_and(row_of == place, slot < live)
    last = jnp.max(jnp.where(named, slot, -1), axis=0, keepdims=True)
    plan_ref[1:2, :] = jnp.where(last < 0, slots, last)


def multiply(coords, plan, adj_v, feat_v, sums):
    def turn(g, carry):
        first = g * UNROLL
        products = [
            jnp.dot(adj_v[first + i], feat_v[coords[1, first + i]], preferred_element_type=F32)
            for i in range(UNROLL)
        ]
        for i in range(UNROLL):
            sums[first + i] = products[i] + sums[plan[0, first + i]]
        return carry

    lax.fori_loop(0, adj_v.shape[0] // UNROLL, turn, 0)


def reduce_rows(p, plan, sums, ysend, yrecv, zsend, zrecv, own_ref, ys_s, ys_r, zs_s, zs_r):
    half = sums.shape[1]

    def part(dy, k, b):
        block_row = (((p.y + dy) % NY) * NH + (p.h + k) % NH) * 2 + b
        return sums[plan[1, block_row]]

    def y_copy(k, dy):
        i = dy - 1
        return remote(ysend.at[k, i], yrecv.at[k, i], ys_s.at[k, i], ys_r.at[k, i], p.at_y(p.y + dy))

    def y_start(k):
        for dy in (2, 1, 3):
            for b in range(2):
                ysend[k, dy - 1, pl.ds(b * half, half)] = part(dy, k, b).astype(BF16)
            y_copy(k, dy).start()

    def y_end(k):
        for dy in range(1, NY):
            y_copy(k, dy).wait_recv()

    def y_sum(k, b):
        total = part(0, k, b)
        for i in range(NY - 1):
            total = total + yrecv[k, i, pl.ds(b * half, half)].astype(F32)
        return total

    def z_copy(i):
        device = p.at_h(p.h + (1 if i % 2 == 0 else NH - 1))
        return remote(zsend.at[i], zrecv.at[i], zs_s.at[i], zs_r.at[i], device)

    def z_start(i, value):
        zsend[i] = value.astype(BF16)
        z_copy(i).start()

    for k in (2, 1, 3, 0):
        y_start(k)
    y_end(2)
    z_start(0, y_sum(2, 0))
    z_start(1, y_sum(2, 1))
    y_end(1)
    z_start(2, y_sum(1, 1))
    y_end(3)
    z_start(3, y_sum(3, 0))
    own_ref[0] = y_sum(1, 0)
    own_ref[1] = y_sum(3, 1)
    z_copy(0).wait_recv()
    z_start(4, own_ref[0] + zrecv[0].astype(F32))
    z_copy(1).wait_recv()
    z_start(5, own_ref[1] + zrecv[1].astype(F32))
    y_end(0)
    own_ref[0] = y_sum(0, 0)
    own_ref[1] = y_sum(0, 1)

    def drain():
        for k in range(NH):
            for dy in range(1, NY):
                y_copy(k, dy).wait_send()
        for i in range(6):
            z_copy(i).wait_send()

    def total(b):
        first, second = ((3, 4), (2, 5))[b]
        z_copy(first).wait_recv()
        z_copy(second).wait_recv()
        return own_ref[b] + zrecv[first].astype(F32) + zrecv[second].astype(F32)

    return total, drain


def silu_slope(preact, sigmoid_value):
    return sigmoid_value * (1.0 + preact * (1.0 - sigmoid_value))


def apply_layer(rounded, weight, cotangent, act_ref, grad_v):
    preact = jnp.dot(rounded, weight, preferred_element_type=F32)
    sigmoid_value = 1.0 / (1.0 + jnp.exp(-preact))
    act_ref[...] = (preact * sigmoid_value).astype(BF16)
    slope_grad = (cotangent.astype(F32) * silu_slope(preact, sigmoid_value)).astype(BF16)
    local_grad = lax.dot_general(rounded, slope_grad, (((0,), (0,)), ((), ())), preferred_element_type=F32)
    members, chunk, lanes = grad_v.shape
    per = members * lanes // local_grad.shape[1]
    for i in range(members // per):
        grad_v[i * per : (i + 1) * per] = local_grad[:, i * lanes : (i + 1) * lanes].reshape(per, chunk, lanes)


def sum_gradient(p, grad_v, r1, c1, r2, c2, r3, c3, r4, g_s, g_r, meanwhile):
    far = p.tall // NEAR

    def all_of(count, k):
        return remote(r1.at[:count], r1.at[:count], g_s.at[k], g_r.at[k], p.member(p.me))

    def scatter(j, carry):
        m = (p.me + j) % p.members
        remote(grad_v.at[m], r1.at[j - 1], g_s.at[0], g_r.at[0], p.member(m)).start()
        return carry

    lax.fori_loop(1, p.members, scatter, 0)
    all_of(p.members - 1, 0).wait_recv()
    c1[...] = grad_v[p.me] + jnp.sum(r1[...], axis=0)
    for j in range(1, NEAR):
        there = p.at_level(p.team * NEAR + (p.near + j) % NEAR)
        remote(c1, r2.at[p.near], g_s.at[1], g_r.at[1], there).start()
    r2[p.near] = c1[...]
    all_of(NEAR - 1, 1).wait_recv()
    c2[...] = jnp.sum(r2[...], axis=0)
    for j in sorted(range(1, far), key=lambda j: -min(j, far - j)):
        remote(c2, r3.at[p.team], g_s.at[2], g_r.at[2], p.up(j * NEAR)).start()
    r3[p.team] = c2[...]
    meanwhile()
    all_of(p.members - 1, 0).wait_send()
    all_of(NEAR - 1, 1).wait_send()
    all_of(far - 1, 2).wait_recv()
    c3[...] = jnp.sum(r3[...], axis=0)

    def hand_out(j, carry):
        remote(c3, r4.at[p.me], g_s.at[3], g_r.at[3], p.member((p.me + j) % p.members)).start()
        return carry

    lax.fori_loop(1, p.members, hand_out, 0)
    r4[p.me] = c3[...]
    all_of(far - 1, 2).wait_send()
    all_of(p.members - 1, 3).wait_recv()
    all_of(p.members - 1, 3).wait_send()


def write_gradient(r4, grad_ref):
    members, chunk, lanes = r4.shape
    per = grad_ref.shape[0] // chunk
    for i in range(members // per):
        grad_ref[:, i * lanes : (i + 1) * lanes] = r4[i * per : (i + 1) * per].reshape(per * chunk, lanes)


def gather_scratch(rows, width):
    dma = pltpu.SemaphoreType.DMA
    return (
        [pltpu.VMEM((2 * NX * NZ * NC, rows // 2, width), BF16)]
        + [dma((NZ, 2))] * 4
        + [dma((2, NZ, 2))] * 2
        + [dma((2, NZ))] * 2
        + [dma((NX, NZ))] * 2
    )


def reduce_scratch(rows, width):
    dma = pltpu.SemaphoreType.DMA
    half = rows // 2
    return (
        [pltpu.VMEM((NH, NY - 1, rows, width), BF16)] * 2
        + [pltpu.VMEM((6, half, width), BF16)] * 2
        + [pltpu.VMEM((2, half, width), F32)]
        + [dma((NH, NY - 1))] * 2
        + [dma((6,))] * 2
    )


def gradient_scratch(size):
    dma = pltpu.SemaphoreType.DMA
    members, lanes = NX * NY * NC, 128
    chunk = (size // members // lanes, lanes)
    return [
        pltpu.VMEM((count,) + chunk if count else chunk, F32)
        for count in (members, members - 1, 0, NEAR, 0, NZ * NH // NEAR, 0, members)
    ] + [dma((4,))] * 2


def whole_kernel(f_ref, adj_ref, coords_ref, counts_ref, w_ref, cot_ref, act_ref, grad_ref, *scratch):
    adj_v, coords_v, coords_s, counts_s, plan_v, plan_s, w_v, cot_v, sums, in_sem, told, feat_v, *rest = scratch
    gather_sems, rest = rest[:10], rest[10:]
    reduce_refs, gradient_refs = rest[:9], rest[9:]
    p = Place()
    slots = adj_v.shape[0]
    pairs = (
        (coords_ref, coords_v), (coords_ref, coords_s), (counts_ref, counts_s), (f_ref, feat_v.at[pl.ds(2 * p.r, 2)]),
        (adj_ref, adj_v), (w_ref, w_v), (cot_ref, cot_v),
    )
    fetches = [pltpu.make_async_copy(a, b, in_sem.at[i]) for i, (a, b) in enumerate(pairs)]
    meet(p)
    gather = Gather(p, f_ref, feat_v, *gather_sems)
    gather.begin()
    tell(p, told.at[0], NEAR)
    for fetch in fetches:
        fetch.start()
    gather.go_on(0, 2)
    hear(p, told.at[0], NEAR)
    tell(p, told.at[1], 2 * NEAR)
    sums[slots] = jnp.zeros(sums.shape[1:], F32)
    for fetch in fetches[:3]:
        fetch.wait()
    find_links(coords_v[...], counts_s[p.c, p.r], plan_v)
    links = pltpu.make_async_copy(plan_v, plan_s, in_sem.at[0])
    links.start()
    gather.go_on(2, NZ)
    links.wait()
    hear(p, told.at[1], 2 * NEAR)
    for fetch in fetches[3:]:
        fetch.wait()
    gather.finish()
    multiply(coords_s, plan_s, adj_v, feat_v, sums)
    total, reduce_drain = reduce_rows(p, plan_s, sums, *reduce_refs)
    rounded = jnp.concatenate([total(0).astype(BF16), total(1).astype(BF16)], axis=0)
    apply_layer(rounded, w_v[...], cot_v[...], act_ref, gradient_refs[0])

    def drain():
        gather.drain()
        reduce_drain()

    sum_gradient(p, *gradient_refs, drain)
    write_gradient(gradient_refs[7], grad_ref)


def body(features, adj_blocks, block_coords, counts, weight, cotangent):
    tile_blocks, tile_coords = adj_blocks[0, 0], block_coords[0, 0]
    slots, block, _ = tile_blocks.shape
    rows, width = features.shape
    dma = pltpu.SemaphoreType.DMA
    vmem, hbm = pl.BlockSpec(memory_space=pltpu.VMEM), pl.BlockSpec(memory_space=pl.ANY)
    return pl.pallas_call(
        whole_kernel,
        out_shape=(
            jax.ShapeDtypeStruct(cotangent.shape, BF16),
            jax.ShapeDtypeStruct(weight.shape, F32),
        ),
        in_specs=[hbm] * 6,
        out_specs=(vmem, vmem),
        scratch_shapes=[
            pltpu.VMEM(tile_blocks.shape, BF16),
            pltpu.VMEM(tile_coords.shape, jnp.int32),
            pltpu.SMEM(tile_coords.shape, jnp.int32),
            pltpu.SMEM(counts.shape[::-1], jnp.int32),
            pltpu.VMEM((2, 128), jnp.int32),
            pltpu.SMEM((2, 128), jnp.int32),
            pltpu.VMEM(weight.shape, BF16),
            pltpu.VMEM(cotangent.shape, BF16),
            pltpu.VMEM((slots + 1, block, width), F32),
            dma((7,)),
            pltpu.SemaphoreType.REGULAR((2,)),
        ]
        + gather_scratch(rows, width)
        + reduce_scratch(rows, width)
        + gradient_scratch(weight.size),
        compiler_params=pltpu.CompilerParams(
            collective_id=0, has_side_effects=True, vmem_limit_bytes=60 << 20
        ),
        name="graph_convolution",
    )(features.reshape(2, rows // 2, width), tile_blocks, tile_coords, counts.T, weight, cotangent)


def solution(mesh):
    return jax.shard_map(
        body,
        mesh=mesh,
        in_specs=(
            P(("col", "row"), None),
            P("row", "col", None, None, None),
            P("row", "col", None, None),
            P(),
            P(),
            P(("row", "col"), None),
        ),
        out_specs=(P(("row", "col"), None), P()),
        check_vma=False,
    )
```

time: 1240 us -> 117 us (0.09)
  waiting for transfers between devices: 1210 us -> 0 us
  Pallas kernels: 0 us -> 113 us
  between operations: 14.4 us -> 0.64 us
    psum x1 -> x0, waiting for transfers between devices: 846 us -> none  [body(): weight_grad = lax.psum(local_grad, ('row', 'col'))]
    reduce_scatter x1 -> x0, waiting for transfers between devices: 221 us -> none  [body(): lax.psum_scatter(partial_rows, 'col', scatter_dimension=0, tiled=True)]
    all_gather x1 -> x0, waiting for transfers between devices: 142 us -> none  [body(): gathered = lax.all_gather(features, 'row', axis=0, tiled=True)]
    pallas_call x0 -> x1, Pallas kernels: none -> 113 us  [body(): pl.pallas_call(whole_kernel, out_shape=(jax.ShapeDtypeStruct(cotangent.sh...]
  transfers between devices with their start and end apart: 3 -> 0, of which waited for: 3 -> 0; matrix products, arithmetic and copies ran while one was open for 0% -> 0% of each run, Pallas kernels for 0% -> 0%
where the time goes in v3:
time: 117 us
  Pallas kernels  113 us (97%)
  local copies, waits for them, and re-layouts  3.14 us (3%)
    pallas_call x1, Pallas kernels, body(): pl.pallas_call(whole_kernel, out_shape=(jax.ShapeDtypeStruct(cotangent.sh...  113 us
    unnamed x2, local copies, waits for them, and re-layouts  3.14 us

profile of v3, /device:TPU:1, one launch (start us, length us, event | category | flops | bytes accessed | tf_op | source)
XLA Modules:
  0.0 116.9 jit_solution(2548679574401247851)
XLA Ops:
  0.6 113.1 %graph_convolution.1 = (bf16[256,256]{1,0:T(8,128)(2,1)}, f32[128,256]{1,0:T(8,128)}) custom-call(bf16[2,128,128]{2,1,0:T(8,128)(2,1)} %bitcast.5, bf16[64,128,128]{2,1,0:T(8,128)(2,1)} %bitcast.4, s32[2,64]{1,0:T(2,128)} %bitcast.7, s32[16,64]{1,0:T(8,128)} %bitcast.6, bf16[128,256]{1,0:T(8,128)(2,1)} %w_ref.1, bf16[256,256]{1,0:T(8,128)(2,1)} %cot_ref.1), custom_call_target="tpu_custom_call" | custom-call | tf_op jit(solution)/shard_map/graph_convolution/pallas_call | solution.py:496
  113.7 1.6 %copy.10 = bf16[256,256]{1,0:T(8,128)(2,1)} copy(bf16[256,256]{1,0:T(8,128)(2,1)} %get-tuple-element.4) | data formatting | bytes 262144
  115.3 1.6 %copy.11 = f32[128,256]{1,0:T(8,128)} copy(f32[128,256]{1,0:T(8,128)} %get-tuple-element.5) | data formatting | bytes 262144

commit v4 on v3

--- a/solution.py
+++ b/solution.py
@@ -8,6 +8,7 @@
 NX, NZ, NC = 4, 8, 2
 NY, NH = 4, 4
 NEAR = 4
+PAIR = 2
 UNROLL = 8
 MESH = pl.DeviceIdType.MESH
 F32, BF16 = jnp.float32, jnp.bfloat16
@@ -33,6 +34,9 @@
     def slot(self, x, z, core=None):
         return ((x % NX) * NZ + z) * NC + (self.core if core is None else core)
 
+    def shelf(self, x, z, core=None):
+        return ((self.core if core is None else core) * NX + x % NX) * NZ + z
+
     def in_column(self, x, z, core=None):
         return {"row": self.slot(x, z, core), "col": self.c}
 
@@ -58,28 +62,27 @@
         return sorted({s % self.tall for s in steps} - {0})
 
 
+def neighbours(p, steps):
+    return [p.at_y(p.y + 1), p.at_y(p.y + NY - 1)] + [p.up(s) for s in p.offsets(steps)]
+
+
 def meet(p):
     barrier = pltpu.get_barrier_semaphore()
-    near = p.offsets(range(-NEAR, NEAR + 1))
-    for s in near:
-        pl.semaphore_signal(barrier, inc=1, device_id=p.up(s), device_id_type=MESH)
-
-    def greet(j, carry):
-        pl.semaphore_signal(barrier, inc=1, device_id=p.member((p.me + j) % p.members), device_id_type=MESH)
-        return carry
-
-    lax.fori_loop(1, p.members, greet, 0)
-    pl.semaphore_wait(barrier, p.members - 1 + len(near))
-
-
-def tell(p, sem, steps):
-    for s in p.offsets((-steps, steps)):
-        pl.semaphore_signal(sem, inc=1, device_id=p.up(s), device_id_type=MESH)
-
-
-def hear(p, sem, steps):
-    if p.offsets((-steps, steps)):
-        pl.semaphore_wait(sem, len(p.offsets((-steps, steps))))
+    devices = neighbours(p, (-NEAR, -1, 1, NEAR)) + [
+        p.in_column(p.x, p.z, 1 - p.core), p.in_column(p.x + 1, p.z), p.in_column(p.x - 1, p.z)
+    ]
+    for device in devices:
+        pl.semaphore_signal(barrier, inc=1, device_id=device, device_id_type=MESH)
+    pl.semaphore_wait(barrier, len(devices))
+
+
+def tell(p, sem):
+    for device in neighbours(p, (-NEAR, NEAR)):
+        pl.semaphore_signal(sem, inc=1, device_id=device, device_id_type=MESH)
+
+
+def hear(p, sem):
+    pl.semaphore_wait(sem, len(neighbours(p, (-NEAR, NEAR))))
 
 
 class Gather:
@@ -96,61 +99,59 @@
         there = self.out_ref.at[2 * s + b]
         return remote(self.f_ref.at[b] if own else there, there, send_sem, recv_sem, device)
 
-    def both(self, s):
-        return self.out_ref.at[pl.ds(2 * s, 2)]
+    def shards(self, s, count=1):
+        return self.out_ref.at[pl.ds(2 * s, 2 * count)]
 
     def z_up(self, d, b, own=False, steps=1):
         k = d + steps - 1
         device = self.p.in_column(self.p.x, self.p.z + steps)
-        return self.send(self.p.slot(self.p.x, self.p.z - d), b, self.zu_s.at[k, b], self.zu_r.at[k, b], device, own)
+        return self.send(self.p.shelf(self.p.x, self.p.z - d), b, self.zu_s.at[k, b], self.zu_r.at[k, b], device, own)
 
     def z_down(self, d, b, own=False, steps=1):
         k = d + steps - 1
         device = self.p.in_column(self.p.x, self.p.z - steps)
-        return self.send(self.p.slot(self.p.x, self.p.z + d), b, self.zd_s.at[k, b], self.zd_r.at[k, b], device, own)
+        return self.send(self.p.shelf(self.p.x, self.p.z + d), b, self.zd_s.at[k, b], self.zd_r.at[k, b], device, own)
 
     def z_up_arrival(self, d, b):
-        s = self.p.slot(self.p.x, self.p.z - d)
+        s = self.p.shelf(self.p.x, self.p.z - d)
         return self.send(s, b, self.zu_s.at[d - 1, b], self.zu_r.at[d - 1, b], self.other)
 
     def z_down_arrival(self, d, b):
-        s = self.p.slot(self.p.x, self.p.z + d)
+        s = self.p.shelf(self.p.x, self.p.z + d)
         return self.send(s, b, self.zd_s.at[d - 1, b], self.zd_r.at[d - 1, b], self.other)
 
-    def x_copy(self, z, way, b, own=False):
+    def x_copy(self, z, way, own=False):
         device = self.right if way == 0 else self.left
-        return self.send(self.p.slot(self.p.x, z), b, self.xs_s.at[way, z, b], self.xs_r.at[way, z, b], device, own)
-
-    def x_arrival(self, z, way, b):
-        s = self.p.slot(self.p.x - 1 if way == 0 else self.p.x + 1, z)
-        return self.send(s, b, self.xs_s.at[way, z, b], self.xs_r.at[way, z, b], self.right)
+        there = self.shards(self.p.shelf(self.p.x, z))
+        return remote(self.f_ref if own else there, there, self.xs_s.at[way, z], self.xs_r.at[way, z], device)
+
+    def x_arrival(self, z, way):
+        here = self.shards(self.p.shelf(self.p.x - 1 if way == 0 else self.p.x + 1, z))
+        return remote(here, here, self.xs_s.at[way, z], self.xs_r.at[way, z], self.right)
 
     def x_forward(self, z, way):
-        s = self.p.slot(self.p.x - 1 if way == 0 else self.p.x + 1, z)
+        s = self.p.shelf(self.p.x - 1 if way == 0 else self.p.x + 1, z)
         device = self.right if way == 0 else self.left
         return self.send(s, way, self.xf_s.at[way, z], self.xf_r.at[way, z], device)
 
     def f_arrival(self, z, way):
-        return self.send(self.p.slot(self.p.x + 2, z), way, self.xf_s.at[way, z], self.xf_r.at[way, z], self.right)
-
-    def cross(self, dx, z, own=False):
-        there = self.both(self.p.slot(self.p.x + dx, z))
-        return remote(self.f_ref if own else there, there, self.cc_s.at[dx, z], self.cc_r.at[dx, z], self.other)
-
-    def cross_arrival(self, dx, z):
-        here = self.both(self.p.slot(self.p.x + dx, z, 1 - self.p.core))
-        return remote(here, here, self.cc_s.at[dx, z], self.cc_r.at[dx, z], self.other)
+        return self.send(self.p.shelf(self.p.x + 2, z), way, self.xf_s.at[way, z], self.xf_r.at[way, z], self.right)
+
+    def cross(self, dx, q, theirs=False):
+        count = PAIR if dx == 2 else NZ // 2
+        core = 1 - self.p.core if theirs else self.p.core
+        there = self.shards(self.p.shelf(self.p.x + dx, q * count, core), count)
+        return remote(there, there, self.cc_s.at[dx, q], self.cc_r.at[dx, q], self.other)
 
     def begin(self):
-        z = self.p.z
         for b in range(2):
             pl.when(self.has_up)(lambda b=b: self.z_up(0, b, True).start())
             pl.when(self.has_down)(lambda b=b: self.z_down(0, b, True).start())
-            self.x_copy(z, 0, b, True).start()
-            self.x_copy(z, 1, 1 - b, True).start()
+        for way in range(2):
+            self.x_copy(self.p.z, way, True).start()
+        for b in range(2):
             pl.when(self.far_up)(lambda b=b: self.z_up(0, b, True, NEAR).start())
             pl.when(self.far_down)(lambda b=b: self.z_down(0, b, True, NEAR).start())
-        self.cross(0, z, True).start()
 
     def along_z(self, d, use):
         z = self.p.z
@@ -162,37 +163,33 @@
             def _():
                 self.z_up_arrival(d, b).wait_recv()
                 pl.when(jnp.logical_and(on, self.has_up))(lambda: self.z_up(d, b).start())
-                self.x_copy(z - d, 0, b).start()
-                self.x_copy(z - d, 1, b).start()
+                if b == 1:
+                    self.x_copy(z - d, 0).start()
+                    self.x_copy(z - d, 1).start()
 
             @pl.when(above)
             def _():
                 self.z_down_arrival(d, b).wait_recv()
                 pl.when(jnp.logical_and(on, self.has_down))(lambda: self.z_down(d, b).start())
-                self.x_copy(z + d, 0, b).start()
-                self.x_copy(z + d, 1, b).start()
-
-        pl.when(below)(lambda: self.cross(0, z - d).start())
-        pl.when(above)(lambda: self.cross(0, z + d).start())
+                if b == 1:
+                    self.x_copy(z + d, 0).start()
+                    self.x_copy(z + d, 1).start()
 
     def along_x(self, z):
         for way in range(2):
-            self.x_arrival(z, way, way).wait_recv()
+            self.x_arrival(z, way).wait_recv()
             self.x_forward(z, way).start()
-        self.x_arrival(z, 0, 1).wait_recv()
-        self.cross(NX - 1, z).start()
-        self.x_arrival(z, 1, 0).wait_recv()
-        self.cross(1, z).start()
-
-    def last_halves(self, z):
-        self.f_arrival(z, 0).wait_recv()
-        self.f_arrival(z, 1).wait_recv()
-        self.cross(2, z).start()
-
-    def at_distance(self, d, act, use=True):
-        z = self.p.z
-        pl.when(jnp.logical_and(use, z - d >= 0))(lambda: act(z - d))
-        pl.when(jnp.logical_and(use, jnp.logical_and(d > 0, z + d < NZ)))(lambda: act(z + d))
+
+    def last_halves(self, q):
+        for i in range(PAIR):
+            for way in range(2):
+                self.f_arrival(q * PAIR + i, way).wait_recv()
+        self.cross(2, q).start()
+
+    def at_distance(self, d, act, use=True, at=None, end=None):
+        at, end = (self.p.z, NZ) if at is None else (at, end)
+        pl.when(jnp.logical_and(use, at - d >= 0))(lambda: act(at - d))
+        pl.when(jnp.logical_and(use, jnp.logical_and(d > 0, at + d < end)))(lambda: act(at + d))
 
     def go_on(self, first, end):
         def distance(k):
@@ -206,32 +203,39 @@
 
         lax.fori_loop(first, end, step, 0)
 
-    def finish(self):
+    def cross_columns(self, act):
+        for dx in (0, 1, NX - 1):
+            for q in range(2):
+                act(dx, q)
+
+    def finish(self, own):
+        own.wait()
+        for q in range(2):
+            self.cross(0, q).start()
         self.at_distance(NZ - 1, self.along_x)
+        for dx in (1, NX - 1):
+            for q in range(2):
+                self.cross(dx, q).start()
 
         def last(d, carry):
-            self.at_distance(d, self.last_halves)
+            self.at_distance(d, self.last_halves, True, self.p.z // PAIR, NZ // PAIR)
             return carry
 
-        lax.fori_loop(0, NZ, last, 0)
-
-        def arrivals(z, carry):
-            for dx in range(NX):
-                self.cross_arrival(dx, z).wait_recv()
-            return carry
-
-        lax.fori_loop(0, NZ, arrivals, 0)
+        lax.fori_loop(0, NZ // PAIR, last, 0)
+        self.cross_columns(lambda dx, q: self.cross(dx, q, True).wait_recv())
+        for q in range(NZ // PAIR):
+            self.cross(2, q, True).wait_recv()
 
     def drain(self):
         z = self.p.z
+        self.cross_columns(lambda dx, q: self.cross(dx, q).wait_send())
+        for q in range(NZ // PAIR):
+            self.cross(2, q).wait_send()
 
         def sent(k, carry):
-            for dx in range(NX):
-                self.cross(dx, k).wait_send()
             for way in range(2):
                 self.x_forward(k, way).wait_send()
-                for b in range(2):
-                    self.x_copy(k, way, b).wait_send()
+                self.x_copy(k, way).wait_send()
             on = jnp.logical_and(k != NEAR - 1, jnp.logical_and(self.has_up, k <= z))
             back = jnp.logical_and(k != NEAR - 1, jnp.logical_and(self.has_down, k <= NZ - 1 - z))
             for b in range(2):
@@ -255,6 +259,9 @@
     before = jnp.max(jnp.where(earlier, down, -1), axis=0, keepdims=True)
     plan_ref[...] = jnp.full(plan_ref.shape, slots, jnp.int32)
     plan_ref[0:1, 0:slots] = jnp.where(before < 0, slots, before)
+    cols = coords[1:2, :]
+    core = (cols // 2) % NC
+    plan_ref[0:1, slots : 2 * slots] = (core * NX * NZ + cols // (2 * NC)) * 2 + cols % 2
     place = lax.broadcasted_iota(jnp.int32, (slots, wide), 1)
     slot = lax.broadcasted_iota(jnp.int32, (slots, wide), 0)
     named = jnp.logical_and(row_of == place, slot < live)
@@ -262,11 +269,11 @@
     plan_ref[1:2, :] = jnp.where(last < 0, slots, last)
 
 
-def multiply(coords, plan, adj_v, feat_v, sums):
+def multiply(plan, adj_v, feat_v, sums):
     def turn(g, carry):
         first = g * UNROLL
         products = [
-            jnp.dot(adj_v[first + i], feat_v[coords[1, first + i]], preferred_element_type=F32)
+            jnp.dot(adj_v[first + i], feat_v[plan[0, adj_v.shape[0] + first + i]], preferred_element_type=F32)
             for i in range(UNROLL)
         ]
         for i in range(UNROLL):
@@ -311,11 +318,13 @@
         zsend[i] = value.astype(BF16)
         z_copy(i).start()
 
-    for k in (2, 1, 3, 0):
-        y_start(k)
+    y_start(2)
+    y_start(1)
     y_end(2)
     z_start(0, y_sum(2, 0))
     z_start(1, y_sum(2, 1))
+    y_start(3)
+    y_start(0)
     y_end(1)
     z_start(2, y_sum(1, 1))
     y_end(3)
@@ -414,9 +423,8 @@
     return (
         [pltpu.VMEM((2 * NX * NZ * NC, rows // 2, width), BF16)]
         + [dma((NZ, 2))] * 4
-        + [dma((2, NZ, 2))] * 2
-        + [dma((2, NZ))] * 2
-        + [dma((NX, NZ))] * 2
+        + [dma((2, NZ))] * 4
+        + [dma((NX, NZ // PAIR))] * 2
     )
 
 
@@ -443,38 +451,37 @@
 
 
 def whole_kernel(f_ref, adj_ref, coords_ref, counts_ref, w_ref, cot_ref, act_ref, grad_ref, *scratch):
-    adj_v, coords_v, coords_s, counts_s, plan_v, plan_s, w_v, cot_v, sums, in_sem, told, feat_v, *rest = scratch
+    adj_v, coords_v, counts_s, plan_v, plan_s, w_v, cot_v, sums, in_sem, told, feat_v, *rest = scratch
     gather_sems, rest = rest[:10], rest[10:]
     reduce_refs, gradient_refs = rest[:9], rest[9:]
     p = Place()
     slots = adj_v.shape[0]
     pairs = (
-        (coords_ref, coords_v), (coords_ref, coords_s), (counts_ref, counts_s), (f_ref, feat_v.at[pl.ds(2 * p.r, 2)]),
+        (coords_ref, coords_v), (counts_ref, counts_s),
+        (f_ref, feat_v.at[pl.ds(2 * p.shelf(p.x, p.z), 2)]),
         (adj_ref, adj_v), (w_ref, w_v), (cot_ref, cot_v),
     )
     fetches = [pltpu.make_async_copy(a, b, in_sem.at[i]) for i, (a, b) in enumerate(pairs)]
     meet(p)
     gather = Gather(p, f_ref, feat_v, *gather_sems)
     gather.begin()
-    tell(p, told.at[0], NEAR)
+    tell(p, told)
     for fetch in fetches:
         fetch.start()
     gather.go_on(0, 2)
-    hear(p, told.at[0], NEAR)
-    tell(p, told.at[1], 2 * NEAR)
     sums[slots] = jnp.zeros(sums.shape[1:], F32)
-    for fetch in fetches[:3]:
+    for fetch in fetches[:2]:
         fetch.wait()
     find_links(coords_v[...], counts_s[p.c, p.r], plan_v)
     links = pltpu.make_async_copy(plan_v, plan_s, in_sem.at[0])
     links.start()
     gather.go_on(2, NZ)
     links.wait()
-    hear(p, told.at[1], 2 * NEAR)
+    hear(p, told)
     for fetch in fetches[3:]:
         fetch.wait()
-    gather.finish()
-    multiply(coords_s, plan_s, adj_v, feat_v, sums)
+    gather.finish(fetches[2])
+    multiply(plan_s, adj_v, feat_v, sums)
     total, reduce_drain = reduce_rows(p, plan_s, sums, *reduce_refs)
     rounded = jnp.concatenate([total(0).astype(BF16), total(1).astype(BF16)], axis=0)
     apply_layer(rounded, w_v[...], cot_v[...], act_ref, gradient_refs[0])
@@ -504,15 +511,14 @@
         scratch_shapes=[
             pltpu.VMEM(tile_blocks.shape, BF16),
             pltpu.VMEM(tile_coords.shape, jnp.int32),
-            pltpu.SMEM(tile_coords.shape, jnp.int32),
             pltpu.SMEM(counts.shape[::-1], jnp.int32),
             pltpu.VMEM((2, 128), jnp.int32),
             pltpu.SMEM((2, 128), jnp.int32),
             pltpu.VMEM(weight.shape, BF16),
             pltpu.VMEM(cotangent.shape, BF16),
             pltpu.VMEM((slots + 1, block, width), F32),
-            dma((7,)),
-            pltpu.SemaphoreType.REGULAR((2,)),
+            dma((6,)),
+            pltpu.SemaphoreType.REGULAR,
         ]
         + gather_scratch(rows, width)
         + reduce_scratch(rows, width)

time: 117 us -> 115 us (0.983)
    pallas_call x1, Pallas kernels: 113 us -> 112 us  [body(): pl.pallas_call(whole_kernel, out_shape=(jax.ShapeDtypeStruct(cotangent.sh...]
where the time goes in v4:
time: 115 us
  Pallas kernels  112 us (97%)
  local copies, waits for them, and re-layouts  3.14 us (3%)
    pallas_call x1, Pallas kernels, body(): pl.pallas_call(whole_kernel, out_shape=(jax.ShapeDtypeStruct(cotangent.sh...  112 us
    unnamed x2, local copies, waits for them, and re-layouts  3.14 us

profile of v4, /device:TPU:1, one launch (start us, length us, event | category | flops | bytes accessed | tf_op | source)
XLA Modules:
  0.0 115.3 jit_solution(10939153696329910181)
XLA Ops:
  0.6 111.5 %graph_convolution.1 = (bf16[256,256]{1,0:T(8,128)(2,1)}, f32[128,256]{1,0:T(8,128)}) custom-call(bf16[2,128,128]{2,1,0:T(8,128)(2,1)} %bitcast.5, bf16[64,128,128]{2,1,0:T(8,128)(2,1)} %bitcast.4, s32[2,64]{1,0:T(2,128)} %bitcast.7, s32[16,64]{1,0:T(8,128)} %bitcast.6, bf16[128,256]{1,0:T(8,128)(2,1)} %w_ref.1, bf16[256,256]{1,0:T(8,128)(2,1)} %cot_ref.1), custom_call_target="tpu_custom_call" | custom-call | tf_op jit(solution)/shard_map/graph_convolution/pallas_call | solution.py:503
  112.2 1.6 %copy.10 = bf16[256,256]{1,0:T(8,128)(2,1)} copy(bf16[256,256]{1,0:T(8,128)(2,1)} %get-tuple-element.4) | data formatting | bytes 262144
  113.7 1.6 %copy.11 = f32[128,256]{1,0:T(8,128)} copy(f32[128,256]{1,0:T(8,128)} %get-tuple-element.5) | data formatting | bytes 262144

commit v5 on v4

--- a/solution.py
+++ b/solution.py
@@ -138,7 +138,7 @@
         return self.send(self.p.shelf(self.p.x + 2, z), way, self.xf_s.at[way, z], self.xf_r.at[way, z], self.right)
 
     def cross(self, dx, q, theirs=False):
-        count = PAIR if dx == 2 else NZ // 2
+        count = NZ // 2 if dx == 0 else PAIR
         core = 1 - self.p.core if theirs else self.p.core
         there = self.shards(self.p.shelf(self.p.x + dx, q * count, core), count)
         return remote(there, there, self.cc_s.at[dx, q], self.cc_r.at[dx, q], self.other)
@@ -175,10 +175,13 @@
                     self.x_copy(z + d, 0).start()
                     self.x_copy(z + d, 1).start()
 
-    def along_x(self, z):
-        for way in range(2):
-            self.x_arrival(z, way).wait_recv()
-            self.x_forward(z, way).start()
+    def along_x(self, q):
+        for i in range(PAIR):
+            for way in range(2):
+                self.x_arrival(q * PAIR + i, way).wait_recv()
+                self.x_forward(q * PAIR + i, way).start()
+        self.cross(NX - 1, q).start()
+        self.cross(1, q).start()
 
     def last_halves(self, q):
         for i in range(PAIR):
@@ -186,10 +189,15 @@
                 self.f_arrival(q * PAIR + i, way).wait_recv()
         self.cross(2, q).start()
 
-    def at_distance(self, d, act, use=True, at=None, end=None):
-        at, end = (self.p.z, NZ) if at is None else (at, end)
-        pl.when(jnp.logical_and(use, at - d >= 0))(lambda: act(at - d))
-        pl.when(jnp.logical_and(use, jnp.logical_and(d > 0, at + d < end)))(lambda: act(at + d))
+    def pairs(self, act):
+        at, end = self.p.z // PAIR, NZ // PAIR
+
+        def step(d, carry):
+            pl.when(at - d >= 0)(lambda: act(at - d))
+            pl.when(jnp.logical_and(d > 0, at + d < end))(lambda: act(at + d))
+            return carry
+
+        lax.fori_loop(0, end, step, 0)
 
     def go_on(self, first, end):
         def distance(k):
@@ -197,40 +205,26 @@
 
         def step(k, carry):
             self.along_z(distance(k), k != NZ - 2)
-            pl.when(k == 1)(lambda: self.along_x(self.p.z))
-            self.at_distance(distance(k - 2), self.along_x, k >= 2)
             return carry
 
         lax.fori_loop(first, end, step, 0)
 
-    def cross_columns(self, act):
-        for dx in (0, 1, NX - 1):
-            for q in range(2):
+    def crossings(self, act):
+        for dx in range(NX):
+            for q in range(2 if dx == 0 else NZ // PAIR):
                 act(dx, q)
 
     def finish(self, own):
         own.wait()
         for q in range(2):
             self.cross(0, q).start()
-        self.at_distance(NZ - 1, self.along_x)
-        for dx in (1, NX - 1):
-            for q in range(2):
-                self.cross(dx, q).start()
-
-        def last(d, carry):
-            self.at_distance(d, self.last_halves, True, self.p.z // PAIR, NZ // PAIR)
-            return carry
-
-        lax.fori_loop(0, NZ // PAIR, last, 0)
-        self.cross_columns(lambda dx, q: self.cross(dx, q, True).wait_recv())
-        for q in range(NZ // PAIR):
-            self.cross(2, q, True).wait_recv()
+        self.pairs(self.along_x)
+        self.pairs(self.last_halves)
+        self.crossings(lambda dx, q: self.cross(dx, q, True).wait_recv())
 
     def drain(self):
         z = self.p.z
-        self.cross_columns(lambda dx, q: self.cross(dx, q).wait_send())
-        for q in range(NZ // PAIR):
-            self.cross(2, q).wait_send()
+        self.crossings(lambda dx, q: self.cross(dx, q).wait_send())
 
         def sent(k, carry):
             for way in range(2):

time: 115 us -> 114 us (level)
  Pallas kernels: 112 us -> 110 us
    pallas_call x1, Pallas kernels: 112 us -> 110 us  [body(): pl.pallas_call(whole_kernel, out_shape=(jax.ShapeDtypeStruct(cotangent.sh...]
where the time goes in v5:
time: 114 us
  Pallas kernels  110 us (96%)
  local copies, waits for them, and re-layouts  3.14 us (3%)
    pallas_call x1, Pallas kernels, body(): pl.pallas_call(whole_kernel, out_shape=(jax.ShapeDtypeStruct(cotangent.sh...  110 us
    unnamed x2, local copies, waits for them, and re-layouts  3.14 us

profile of v5, /device:TPU:1, one launch (start us, length us, event | category | flops | bytes accessed | tf_op | source)
XLA Modules:
  0.0 113.6 jit_solution(6424250393620294487)
XLA Ops:
  0.6 109.8 %graph_convolution.1 = (bf16[256,256]{1,0:T(8,128)(2,1)}, f32[128,256]{1,0:T(8,128)}) custom-call(bf16[2,128,128]{2,1,0:T(8,128)(2,1)} %bitcast.5, bf16[64,128,128]{2,1,0:T(8,128)(2,1)} %bitcast.4, s32[2,64]{1,0:T(2,128)} %bitcast.7, s32[16,64]{1,0:T(8,128)} %bitcast.6, bf16[128,256]{1,0:T(8,128)(2,1)} %w_ref.1, bf16[256,256]{1,0:T(8,128)(2,1)} %cot_ref.1), custom_call_target="tpu_custom_call" | custom-call | tf_op jit(solution)/shard_map/graph_convolution/pallas_call | solution.py:497
  110.5 1.6 %copy.10 = bf16[256,256]{1,0:T(8,128)(2,1)} copy(bf16[256,256]{1,0:T(8,128)(2,1)} %get-tuple-element.4) | data formatting | bytes 262144
  112.0 1.6 %copy.11 = f32[128,256]{1,0:T(8,128)} copy(f32[128,256]{1,0:T(8,128)} %get-tuple-element.5) | data formatting | bytes 262144

commit v6 on v5

--- a/solution.py
+++ b/solution.py
@@ -9,7 +9,7 @@
 NY, NH = 4, 4
 NEAR = 4
 PAIR = 2
-UNROLL = 8
+UNROLL = 16
 MESH = pl.DeviceIdType.MESH
 F32, BF16 = jnp.float32, jnp.bfloat16
 

time: 114 us -> 113 us (level)
  no operation moved by 1% of the time
where the time goes in v6:
time: 113 us
  Pallas kernels  109 us (96%)
  local copies, waits for them, and re-layouts  3.14 us (3%)
    pallas_call x1, Pallas kernels, body(): pl.pallas_call(whole_kernel, out_shape=(jax.ShapeDtypeStruct(cotangent.sh...  109 us
    unnamed x2, local copies, waits for them, and re-layouts  3.14 us

profile of v6, /device:TPU:1, one launch (start us, length us, event | category | flops | bytes accessed | tf_op | source)
XLA Modules:
  0.0 112.9 jit_solution(6581538170485168762)
XLA Ops:
  0.6 109.1 %graph_convolution.1 = (bf16[256,256]{1,0:T(8,128)(2,1)}, f32[128,256]{1,0:T(8,128)}) custom-call(bf16[2,128,128]{2,1,0:T(8,128)(2,1)} %bitcast.5, bf16[64,128,128]{2,1,0:T(8,128)(2,1)} %bitcast.4, s32[2,64]{1,0:T(2,128)} %bitcast.7, s32[16,64]{1,0:T(8,128)} %bitcast.6, bf16[128,256]{1,0:T(8,128)(2,1)} %w_ref.1, bf16[256,256]{1,0:T(8,128)(2,1)} %cot_ref.1), custom_call_target="tpu_custom_call" | custom-call | tf_op jit(solution)/shard_map/graph_convolution/pallas_call | solution.py:497
  109.7 1.6 %copy.10 = bf16[256,256]{1,0:T(8,128)(2,1)} copy(bf16[256,256]{1,0:T(8,128)(2,1)} %get-tuple-element.4) | data formatting | bytes 262144
  111.3 1.6 %copy.11 = f32[128,256]{1,0:T(8,128)} copy(f32[128,256]{1,0:T(8,128)} %get-tuple-element.5) | data formatting | bytes 262144
